TPU v7x, 32 devices: a whole 2x2x4 slice. The times are simulated.
32 devices in a mesh: gx: 4 (over y, core), gy: 2 (over x), gz: 4 (over z).
Axes of the slice: x: 2, y: 2, z: 4, core: 2. Of those that a mesh axis runs over, the one named last changes fastest.
Arguments:
- tokens: bfloat16 [32, 16, 32, 256], P('gx', 'gy', 'gz'), may hold values from -6 to 6
- norm_gain: float32 [256], replicated, may hold values from 0.5 to 1.5
- query_weight: bfloat16 [256, 256], replicated, may hold values from -2 to 2
- key_weight: bfloat16 [256, 256], replicated, may hold values from -2 to 2
- value_weight: bfloat16 [256, 256], replicated, may hold values from -0.375 to 0.375
- head_scale: float32 [8], replicated, may hold values from 1 to 6
- out_weight: bfloat16 [256, 256], replicated, may hold values from -0.375 to 0.375
- mlp_gain: float32 [256], replicated, may hold values from 0.5 to 1.5
- up_weight: bfloat16 [256, 512], replicated, may hold values from -0.375 to 0.375
- down_weight: bfloat16 [512, 256], replicated, may hold values from -0.25 to 0.25
Outputs:
- layer_out: bfloat16 [32, 16, 32, 256], P('gx', 'gy', 'gz')
All inputs are finite; a program needn't handle non-finite values.
Results may differ from a plain program's by a relative error of at most 0.0095.
Values may be sent and summed in bfloat16 or wider, within the bound.
No kernel may reach another device: no remote copies, remote signals or barrier semaphores. Data moves between devices by JAX's collectives and lax.ppermute only.
A program may use at most 128 MiB of HBM per device.

v0:
```python
import functools
import math

import jax
import jax.numpy as jnp
import numpy as np
from jax import lax
from jax.experimental import pallas as pl
from jax.experimental.pallas import tpu as pltpu
from jax.sharding import PartitionSpec as P

HEADS = 8
EPSILON = 1e-05
LOG2E = 1.4426950408889634
NEGATIVE = -1e30
LANES = 128
F32 = jnp.float32
BF16 = jnp.bfloat16
AXES = ("gx", "gy", "gz")


def up_to(count, step):
    return -(-count // step) * step


def in_vmem(array):
    return pltpu.with_memory_space_constraint(array, pltpu.VMEM)


def layer_norm(values, gain):
    average = jnp.mean(values, axis=-1, keepdims=True)
    centered = values - average
    variance = jnp.mean(centered * centered, axis=-1, keepdims=True)
    return (centered * lax.rsqrt(variance + EPSILON) * gain).astype(BF16)


def dot(left, right):
    return jnp.dot(left, right, preferred_element_type=F32)


def dot_nt(left, right):
    return lax.dot_general(left, right, (((1,), (1,)), ((), ())), preferred_element_type=F32)


def dot_tn(left, right):
    return lax.dot_general(left, right, (((0,), (0,)), ((), ())), preferred_element_type=F32)


def joined(ref, rows):
    return jnp.concatenate([ref[j, rows, :] for j in range(ref.shape[0])], axis=1)


def call(kernel, outs, *args, scratch=(), vmem=True, limit=24 << 20):
    kinds = [pltpu.VMEM(s, d) if vmem else jax.ShapeDtypeStruct(s, d) for s, d in outs]
    return pl.pallas_call(
        kernel,
        out_shape=kinds,
        in_specs=[
            pl.BlockSpec(memory_space=pltpu.SMEM)
            if a.dtype == jnp.int32
            else pl.BlockSpec(memory_space=pltpu.VMEM)
            for a in args
        ],
        out_specs=[pl.BlockSpec(memory_space=pltpu.VMEM) for _ in outs],
        scratch_shapes=list(scratch),
        compiler_params=pltpu.CompilerParams(vmem_limit_bytes=limit),
    )(*args)


class Sizes:
    def __init__(self, extent, channels):
        self.x, self.y, self.z = extent
        self.c = channels
        self.parts = channels // LANES
        self.cells = self.x * self.y * self.z
        self.mx, self.my, self.mz = (n // 2 for n in extent)
        self.mids = self.mx * self.my * self.mz
        self.coarse = self.mids // 8
        self.zp = up_to(self.z + 2, 16)
        self.mzp = up_to(self.mz + 2, 8)
        self.fine_rows = (self.x + 2) * (self.y + 2) * self.zp
        self.mid_rows = (self.mx + 2) * (self.my + 2) * self.mzp
        self.fx, self.gx = self.y * self.z, self.my * self.mz
        self.fy, self.gy = (self.x + 2) * self.z, (self.mx + 2) * self.mz
        self.fz, self.gz = (self.x + 2) * (self.y + 2), (self.mx + 2) * (self.my + 2)


def pooling(size):
    x, y, z = np.unravel_index(np.arange(size.cells), (size.x, size.y, size.z))
    middle = ((x // 2) * size.my + y // 2) * size.mz + z // 2
    coarse = ((x // 4) * (size.my // 2) + y // 4) * (size.mz // 2) + z // 4
    rows = np.zeros((size.mids + up_to(size.coarse, 16), size.cells), np.float32)
    rows[middle, np.arange(size.cells)] = 1.0
    rows[size.mids + coarse, np.arange(size.cells)] = 1.0
    return rows.astype(jnp.bfloat16)


def window_bias(length, padded, query_cells, factor, z_cells):
    place = np.arange(padded)
    key = np.where(place < length, place, np.where(place == length, -1, length))
    query_z = np.arange(query_cells) % z_cells
    start = 2 * (query_z // factor)
    seen = (key[:, None] >= start - 1) & (key[:, None] <= start + 2) & (place[:, None] < length + 2)
    bias = np.where(seen, 0.0, NEGATIVE).astype(np.float32)
    return np.tile(bias, (1, HEADS))


def first_kernel(size, odd, tokens, gain, pool, normed, middle, face_a, face_b, coarse_out):
    values = layer_norm(tokens[...].astype(F32), gain[...])
    normed[...] = values
    pooled = dot(pool[...], values)
    mids = (pooled[: size.mids] * 0.125).astype(BF16)
    middle[...] = mids
    coarse_out[...] = (pooled[size.mids :] * (1.0 / 64.0)).astype(BF16)
    high = jnp.concatenate([values[size.cells - size.fx :], mids[size.mids - size.gx :]], axis=0)
    low = jnp.concatenate([values[: size.fx], mids[: size.gx]], axis=0)
    is_odd = odd[0] == 1
    face_a[...] = jnp.where(is_odd, low, high)
    face_b[...] = jnp.where(is_odd, high, low)


def pick(odd, from_a, from_b):
    is_odd = odd == 1
    first, second = from_a[...].astype(F32), from_b[...].astype(F32)
    return jnp.where(is_odd, first, second), jnp.where(is_odd, second, first)


def y_kernel(size, odd, normed, middle, from_a, from_b, face):
    low, high = pick(odd[0], from_a, from_b)
    cells = normed[...].astype(F32).reshape(size.x, size.y, size.z, size.c)
    mids = middle[...].astype(F32).reshape(size.mx, size.my, size.mz, size.c)
    parts = []
    for at, mat in ((0, 0), (size.y - 1, size.my - 1)):
        fine_low = low[: size.fx].reshape(size.y, size.z, size.c)[at]
        fine_high = high[: size.fx].reshape(size.y, size.z, size.c)[at]
        mid_low = low[size.fx :].reshape(size.my, size.mz, size.c)[mat]
        mid_high = high[size.fx :].reshape(size.my, size.mz, size.c)[mat]
        own = cells[:, at].reshape(size.x * size.z, size.c)
        own_mid = mids[:, mat].reshape(size.mx * size.mz, size.c)
        parts.append(
            jnp.concatenate([fine_low, own, fine_high, mid_low, own_mid, mid_high], axis=0)
        )
    face[...] = jnp.concatenate(parts, axis=0).astype(BF16)


def fill(size, odd_x, normed, middle, from_a, from_b, y_low, y_high, fine, mid):
    low, high = pick(odd_x, from_a, from_b)
    fine[...] = jnp.zeros_like(fine)
    mid[...] = jnp.zeros_like(mid)
    cells = normed[...].astype(F32)
    mids = middle[...].astype(F32)

    def put(x, y, run):
        at = (x * (size.y + 2) + y) * size.zp
        for j in range(size.parts):
            fine[j, at : at + size.z, :] = run[:, j * LANES : (j + 1) * LANES]

    def put_mid(x, y, run):
        at = (x * (size.my + 2) + y) * size.mzp
        for j in range(size.parts):
            mid[j, at : at + size.mz, :] = run[:, j * LANES : (j + 1) * LANES]

    for x in range(size.x):
        for y in range(size.y):
            at = (x * size.y + y) * size.z
            put(x + 1, y + 1, cells[at : at + size.z])
    for x in range(size.mx):
        for y in range(size.my):
            at = (x * size.my + y) * size.mz
            put_mid(x + 1, y + 1, mids[at : at + size.mz])
    for x, halo in ((0, low), (size.x + 1, high)):
        for y in range(size.y):
            put(x, y + 1, halo[y * size.z : (y + 1) * size.z])
    for x, halo in ((0, low), (size.mx + 1, high)):
        for y in range(size.my):
            put_mid(x, y + 1, halo[size.fx + y * size.mz : size.fx + (y + 1) * size.mz])
    for y, my, halo in ((0, 0, y_low), (size.y + 1, size.my + 1, y_high)):
        for x in range(size.x + 2):
            put(x, y, halo[x * size.z : (x + 1) * size.z])
        for x in range(size.mx + 2):
            put_mid(x, my, halo[size.fy + x * size.mz : size.fy + (x + 1) * size.mz])


def z_kernel(size, pair, odd, normed, middle, from_a, from_b, *refs):
    y_refs, (face_a, face_b, fine, mid) = refs[: 1 if pair else 2], refs[1 if pair else 2 :]
    half = size.fy + size.gy
    if pair:
        both = y_refs[0][...].astype(F32)
        y_low, y_high = both[half:], both[:half]
    else:
        y_low = y_refs[0][...].astype(F32)
        y_high = y_refs[1][...].astype(F32)
    fill(size, odd[0], normed, middle, from_a, from_b, y_low, y_high, fine, mid)

    def cut(z, mz):
        return jnp.concatenate(
            [
                joined(fine, pl.ds(z, size.fz, stride=size.zp)),
                joined(mid, pl.ds(mz, size.gz, stride=size.mzp)),
            ],
            axis=0,
        )

    low, high = cut(0, 0), cut(size.z - 1, size.mz - 1)
    is_odd = odd[1] == 1
    face_a[...] = jnp.where(is_odd, low, high).astype(BF16)
    face_b[...] = jnp.where(is_odd, high, low).astype(BF16)


def last_kernel(
    size,
    coarse_rows,
    n_coarse,
    odd,
    scale,
    tokens,
    fine,
    mid,
    from_a,
    from_b,
    query_weight,
    key_weight,
    value_weight,
    out_weight,
    mlp_gain,
    up_weight,
    down_weight,
    fine_bias,
    mid_bias,
    mask,
    *refs,
):
    coarse_refs, (out, fine_pad, mid_pad, keys, values, queries, attended) = refs[:n_coarse], refs[n_coarse:]
    low, high = pick(odd[1], from_a, from_b)
    fine_pad[...] = fine[...]
    mid_pad[...] = mid[...]
    for j in range(size.parts):
        lanes = slice(j * LANES, (j + 1) * LANES)
        fine_pad[j, pl.ds(size.z, size.fz, stride=size.zp), :] = low[: size.fz, lanes]
        fine_pad[j, pl.ds(size.z + 1, size.fz, stride=size.zp), :] = high[: size.fz, lanes]
        mid_pad[j, pl.ds(size.mz, size.gz, stride=size.mzp), :] = low[size.fz :, lanes]
        mid_pad[j, pl.ds(size.mz + 1, size.gz, stride=size.mzp), :] = high[size.fz :, lanes]

    whole = joined(fine_pad, slice(None))
    sources = [whole.astype(BF16), joined(mid_pad, slice(None)).astype(BF16)]
    sources.append(jnp.concatenate([r[...] for r in coarse_refs], axis=0))
    cells = jnp.concatenate(sources, axis=0)
    keys[...] = dot(cells, key_weight[...]).astype(BF16)
    values[...] = dot(cells, value_weight[...]).astype(BF16)
    own = whole.reshape(size.x + 2, size.y + 2, size.zp, size.c)
    own = own[1 : size.x + 1, 1 : size.y + 1, : size.z].reshape(size.cells, size.c)
    queries[...] = dot(own.astype(BF16), query_weight[...]).astype(BF16)

    mid_at = size.fine_rows
    coarse_at = mid_at + size.mid_rows
    run = 2 * size.z
    group = 2 * run
    fine_row = (size.y + 2) * size.zp
    mid_row = (size.my + 2) * size.mzp

    def weigh(scores, bias, length):
        scores = scores * scale[...]
        if bias is not None:
            scores = (scores.reshape(-1, length, scores.shape[-1]) + bias[...][None]).reshape(scores.shape)
        weights = jnp.exp2(scores - jnp.max(scores, axis=0, keepdims=True))
        return (weights * (1.0 / jnp.sum(weights, axis=0, keepdims=True))).astype(BF16)

    groups_y = size.y // 2

    def one_group(index, carry):
        bx, by = index // groups_y, index % groups_y
        rows = [
            pl.ds(pl.multiple_of(((2 * bx + dx) * size.y + 2 * by) * size.z, 16), run) for dx in (0, 1)
        ]
        some = jnp.concatenate([queries[r, :] for r in rows], axis=0)
        spread = jnp.concatenate([some] * HEADS, axis=0) * mask[...]
        fine_slabs = [
            pl.ds(pl.multiple_of((2 * bx + k) * fine_row + 2 * by * size.zp, 16), 4 * size.zp)
            for k in range(4)
        ]
        mid_slabs = [
            pl.ds(
                pl.multiple_of(
                    mid_at + (2 * (bx // 2) + k) * mid_row + 2 * (by // 2) * size.mzp, 16
                ),
                4 * size.mzp,
            )
            for k in range(4)
        ]
        coarse_slabs = [pl.ds(coarse_at, coarse_rows)]
        total = None
        for slabs, bias, length in (
            (fine_slabs, fine_bias, size.zp),
            (mid_slabs, mid_bias, size.mzp),
            (coarse_slabs, None, 0),
        ):
            some_keys = jnp.concatenate([keys[s, :] for s in slabs], axis=0)
            some_values = jnp.concatenate([values[s, :] for s in slabs], axis=0)
            weights = weigh(dot_nt(some_keys, spread), bias, length)
            part = dot_tn(weights, some_values)
            total = part if total is None else total + part
        total = total.reshape(HEADS, group, size.c)
        wide = mask[...].astype(F32).reshape(HEADS, group, size.c)
        result = jnp.sum(total * wide, axis=0).astype(BF16)
        for k, r in enumerate(rows):
            attended[r, :] = result[k * run : (k + 1) * run]
        return carry

    lax.fori_loop(0, (size.x // 2) * groups_y, one_group, 0, unroll=True)
    residual = (tokens[...].astype(F32) + dot(attended[...], out_weight[...])).astype(BF16)
    second = layer_norm(residual.astype(F32), mlp_gain[...])
    hidden = jax.nn.gelu(dot(second, up_weight[...]), approximate=True).astype(BF16)
    out[...] = (residual.astype(F32) + dot(hidden, down_weight[...])).astype(BF16)


def swap(array, axis, start):
    count = lax.axis_size(axis)
    pairs = []
    for i in range(start, count, 2):
        other = (i + 1) % count
        pairs += [(i, other), (other, i)]
    return lax.ppermute(array, axis, pairs)


def shift(array, axis, by):
    count = lax.axis_size(axis)
    return lax.ppermute(array, axis, [(i, (i + by) % count) for i in range(count)])


def shards(
    tokens,
    norm_gain,
    query_weight,
    key_weight,
    value_weight,
    head_scale,
    out_weight,
    mlp_gain,
    up_weight,
    down_weight,
):
    channels = tokens.shape[-1]
    size = Sizes(tokens.shape[:3], channels)
    nx, ny, nz = (lax.axis_size(a) for a in AXES)
    flat = tokens.reshape(size.cells, channels)
    odd = jnp.stack([lax.axis_index("gx") % 2, lax.axis_index("gz") % 2]).astype(jnp.int32)
    coarse_rows = up_to(size.coarse, 16)

    fx, gx, fy, gy, fz, gz = size.fx, size.gx, size.fy, size.gy, size.fz, size.gz
    normed, middle, face_a, face_b, coarse = call(
        functools.partial(first_kernel, size),
        [
            ((size.cells, channels), BF16),
            ((size.mids, channels), BF16),
            ((fx + gx, channels), BF16),
            ((fx + gx, channels), BF16),
            ((coarse_rows, channels), BF16),
        ],
        odd,
        flat,
        norm_gain.reshape(1, -1),
        jnp.asarray(pooling(size)),
    )
    from_a = in_vmem(swap(face_a, "gx", 0))
    from_b = in_vmem(swap(face_b, "gx", 1))
    faces = call(
        functools.partial(y_kernel, size),
        [((2 * (fy + gy), channels), BF16)],
        odd,
        normed,
        middle,
        from_a,
        from_b,
    )[0]
    if ny == 2:
        from_y = [in_vmem(swap(faces, "gy", 0))]
    else:
        from_y = [
            in_vmem(shift(faces[fy + gy :], "gy", 1)),
            in_vmem(shift(faces[: fy + gy], "gy", -1)),
        ]
    z_a, z_b, fine, mid = call(
        functools.partial(z_kernel, size, ny == 2),
        [
            ((fz + gz, channels), BF16),
            ((fz + gz, channels), BF16),
            ((size.parts, size.fine_rows, LANES), F32),
            ((size.parts, size.mid_rows, LANES), F32),
        ],
        odd,
        normed,
        middle,
        from_a,
        from_b,
        *from_y,
    )
    got_a = in_vmem(swap(z_a, "gz", 0))
    got_b = in_vmem(swap(z_b, "gz", 1))
    gathered = lax.all_to_all(
        jnp.broadcast_to(coarse[None, : size.coarse], (nx * ny * nz, size.coarse, channels)), AXES, 0, 0
    ).reshape(-1, channels)

    total_coarse = gathered.shape[0]
    key_rows = size.fine_rows + size.mid_rows + total_coarse
    group = 4 * size.z
    head = np.arange(HEADS * group) // group
    mask = (head[:, None] == np.arange(channels)[None, :] // (channels // HEADS)).astype(jnp.bfloat16)
    scale = jnp.repeat(head_scale * (LOG2E / math.sqrt(channels // HEADS)), group).reshape(1, -1)
    out = call(
        functools.partial(last_kernel, size, total_coarse, 1),
        [((size.cells, channels), BF16)],
        odd,
        scale,
        flat,
        fine,
        mid,
        got_a,
        got_b,
        query_weight,
        key_weight,
        value_weight,
        out_weight,
        mlp_gain.reshape(1, -1),
        up_weight,
        down_weight,
        jnp.asarray(window_bias(size.z, size.zp, group, 2, size.z)),
        jnp.asarray(window_bias(size.mz, size.mzp, group, 4, size.z)),
        jnp.asarray(mask),
        gathered,
        scratch=[
            pltpu.VMEM((size.parts, size.fine_rows, LANES), F32),
            pltpu.VMEM((size.parts, size.mid_rows, LANES), F32),
            pltpu.VMEM((key_rows, channels), BF16),
            pltpu.VMEM((key_rows, channels), BF16),
            pltpu.VMEM((size.cells, channels), BF16),
            pltpu.VMEM((size.cells, channels), BF16),
        ],
        vmem=False,
    )[0]
    return out.reshape(tokens.shape)


def solution(mesh):
    in_specs = (P("gx", "gy", "gz", None), P(), P(), P(), P(), P(), P(), P(), P(), P())
    out_specs = P("gx", "gy", "gz", None)
    return jax.shard_map(shards, mesh=mesh, in_specs=in_specs, out_specs=out_specs, check_vma=False)
```

profile of v0, /device:TPU:0, one launch (start us, length us, event | category | flops | bytes accessed | tf_op | source)
XLA Modules:
  0.0 41.3 jit_solution(4393501139831311805)
XLA Ops:
  0.0 0.0 copy-start.15
  0.0 0.0 copy-start.18
  0.0 0.0 copy-start.17
  0.0 0.1 pad_add_fusion.odd
  0.1 0.0 copy-start
  0.1 0.9 %copy-done = bf16[8,8,8,256]{3,2,1,0:T(8,128)(2,1)S(1)} copy-done((bf16[8,8,8,256]{3,2,1,0:T(8,128)(2,1)S(1)}, bf16[8,8,8,256]{3,2,1,0:T(8,128)(2,1)}, u32[]{:S(2)}) %copy-start) | copy-done | bytes 262168
  1.0 0.0 copy-start.11
  1.0 0.9 %copy-done.11 = bf16[80,512]{1,0:T(8,128)(2,1)S(1)} copy-done((bf16[80,512]{1,0:T(8,128)(2,1)S(1)}, bf16[80,512]{1,0:T(8,128)(2,1)}, u32[]{:S(2)}) %copy-start.11) | copy-done | bytes 81944
  1.9 0.0 copy-start.16
  1.9 0.7 %copy-done.16 = f32[256]{0:T(256)S(1)} copy-done((f32[256]{0:T(256)S(1)}, f32[256]{0:T(256)}, u32[]{:S(2)}) %copy-start.16) | copy-done | bytes 1048
  2.6 0.0 copy-start.5
  2.6 0.9 %shard_map.136 = (bf16[512,256]{1,0:T(8,128)(2,1)S(1)}, bf16[64,256]{1,0:T(8,128)(2,1)S(1)}, bf16[80,256]{1,0:T(8,128)(2,1)S(1)}, bf16[80,256]{1,0:T(8,128)(2,1)S(1)}, bf16[16,256]{1,0:T(8,128)(2,1)S(1)}) custom-call(s32[2]{0:T(128)S(1)} %pad_add_fusion.odd, bf16[512,256]{1,0:T(8,128)(2,1)S(1)} %bitcast.7, f32[1,256]{1,0:T(1,128)S(1)} %bitcast.10, ...), custom_call_target="tpu_custom_call" | custom-call | tf_op jit(solution)/shard_map/pallas_call | solution.py:55
  3.6 0.5 %collective-permute-start = (bf16[80,256]{1,0:T(8,128)(2,1)S(1)}, bf16[80,256]{1,0:T(8,128)(2,1)S(1)}, u32[]{:S(2)}, u32[]{:S(2)}) collective-permute-start(bf16[80,256]{1,0:T(8,128)(2,1)S(1)} %get-tuple-element.16), channel_id=1, source_target_pairs={{0,8},{8,0},{16,24},{24,16},{1,9},{9,1},{17,25},{25,17},{2,10},{10... | collective-permute-start | bytes 122888 | tf_op jit(solution)/shard_map/ppermute | solution.py:322
  4.1 2.6 %collective-permute-start.1 = (bf16[80,256]{1,0:T(8,128)(2,1)S(1)}, bf16[80,256]{1,0:T(8,128)(2,1)S(1)}, u32[]{:S(2)}, u32[]{:S(2)}) collective-permute-start(bf16[80,256]{1,0:T(8,128)(2,1)S(1)} %get-tuple-element.17), channel_id=1, source_target_pairs={{8,16},{16,8},{24,0},{0,24},{9,17},{17,9},{25,1},{1,25},{10,18},{1... | collective-permute-start | bytes 122888 | tf_op jit(solution)/shard_map/ppermute | solution.py:322
  6.7 0.0 collective-permute-done.from_a
  6.7 1.8 %collective-permute-done.1.from_b = bf16[80,256]{1,0:T(8,128)(2,1)S(1)} collective-permute-done((bf16[80,256]{1,0:T(8,128)(2,1)S(1)}, bf16[80,256]{1,0:T(8,128)(2,1)S(1)}, u32[]{:S(2)}, u32[]{:S(2)}) %collective-permute-start.1) | collective-permute-done | bytes 40992 | tf_op jit(solution)/shard_map/ppermute | solution.py:322
  8.6 0.6 %shard_map.137 = bf16[208,256]{1,0:T(8,128)(2,1)S(1)} custom-call(s32[2]{0:T(128)S(1)} %pad_add_fusion.odd, bf16[512,256]{1,0:T(8,128)(2,1)S(1)} %get-tuple-element.14.normed, bf16[64,256]{1,0:T(8,128)(2,1)S(1)} %get-tuple-element.15.middle, bf16[80,256]{1,0:T(8,128)(2,1)S(1)} %collective-permute-done.from_a, bf16[80,256]{1,0:T(8,128)(2,1)S(1)} %collective-permute-done.1.from_b), custom_call_target="tpu_custom_call" | custom-call | tf_op jit(solution)/shard_map/pallas_call | solution.py:55
  9.2 1.6 %collective-permute-start.2 = (bf16[208,256]{1,0:T(8,128)(2,1)S(1)}, bf16[208,256]{1,0:T(8,128)(2,1)S(1)}, u32[]{:S(2)}, u32[]{:S(2)}) collective-permute-start(bf16[208,256]{1,0:T(8,128)(2,1)S(1)} %shard_map.137), channel_id=1, source_target_pairs={{0,4},{4,0},{1,5},{5,1},{2,6},{6,2},{3,7},{7,3},{8,12},{12,8},{9,1... | collective-permute-start | bytes 319496 | tf_op jit(solution)/shard_map/ppermute | solution.py:322
  10.7 0.7 %broadcast_in_dim.10 = bf16[32,8,256]{2,1,0:T(8,128)(2,1)} broadcast(bf16[8,256]{1,0:T(8,128)(2,1)S(1)} %slice.3), dimensions={1,2} | broadcast | bytes 135168 | tf_op jit(solution)/shard_map/broadcast_in_dim | solution.py:400
  11.4 4.9 %all-to-all-start = ((bf16[32,8,256]{2,1,0:T(8,128)(2,1)}), bf16[32,8,256]{2,1,0:T(8,128)(2,1)S(1)}, u32[]{:S(2)}, u32[]{:S(2)}) async-start(bf16[32,8,256]{2,1,0:T(8,128)(2,1)} %broadcast_in_dim.10), calls=%async_computation | async-start | bytes 262144 | tf_op jit(solution)/shard_map/all_to_all | solution.py:399
  16.3 0.0 collective-permute-done.2.refs_0_
  16.3 0.0 copy-start.9
  16.3 0.6 %copy-done.9 = bf16[208,256]{1,0:T(8,128)(2,1)} copy-done((bf16[208,256]{1,0:T(8,128)(2,1)}, bf16[208,256]{1,0:T(8,128)(2,1)S(1)}, u32[]{:S(2)}) %copy-start.9) | copy-done | bytes 106520
  17.0 0.9 %copy-done.10 = bf16[208,256]{1,0:T(8,128)(2,1)S(1)} copy-done((bf16[208,256]{1,0:T(8,128)(2,1)S(1)}, bf16[208,256]{1,0:T(8,128)(2,1)}, u32[]{:S(2)}) %copy-start.10) | copy-done | bytes 106520
  17.9 1.5 %shard_map.138 = (bf16[136,256]{1,0:T(8,128)(2,1)}, bf16[136,256]{1,0:T(8,128)(2,1)}, f32[2,1600,128]{2,1,0:T(8,128)S(1)}, f32[2,288,128]{2,1,0:T(8,128)S(1)}) custom-call(s32[2]{0:T(128)S(1)} %pad_add_fusion.odd, bf16[512,256]{1,0:T(8,128)(2,1)S(1)} %get-tuple-element.14.normed, bf16[64,256]{1,0:T(8,128)(2,1)S(1)} %get-tuple-element.15.middle, ...), custom_call_target="tpu_custom_call" | custom-call | tf_op jit(solution)/shard_map/pallas_call | solution.py:55
  19.3 1.8 %collective-permute-start.3 = (bf16[136,256]{1,0:T(8,128)(2,1)}, bf16[136,256]{1,0:T(8,128)(2,1)S(1)}, u32[]{:S(2)}, u32[]{:S(2)}) collective-permute-start(bf16[136,256]{1,0:T(8,128)(2,1)} %get-tuple-element.20), channel_id=1, source_target_pairs={{0,1},{1,0},{2,3},{3,2},{4,5},{5,4},{6,7},{7,6},{8,9},{9,8},{10,11... | collective-permute-start | bytes 208904 | tf_op jit(solution)/shard_map/ppermute | solution.py:322
  21.1 2.4 %collective-permute-start.4 = (bf16[136,256]{1,0:T(8,128)(2,1)}, bf16[136,256]{1,0:T(8,128)(2,1)S(1)}, u32[]{:S(2)}, u32[]{:S(2)}) collective-permute-start(bf16[136,256]{1,0:T(8,128)(2,1)} %get-tuple-element.21), channel_id=1, source_target_pairs={{1,2},{2,1},{3,0},{0,3},{5,6},{6,5},{7,4},{4,7},{9,10},{10,9},{11,... | collective-permute-start | bytes 208904 | tf_op jit(solution)/shard_map/ppermute | solution.py:322
  23.5 0.0 copy-done.18
  23.5 0.1 broadcast_in_dim.4
  23.6 0.1 reshape_reshape.3.scale
  23.6 0.5 %collective-permute-done.3.from_a = bf16[136,256]{1,0:T(8,128)(2,1)S(1)} collective-permute-done((bf16[136,256]{1,0:T(8,128)(2,1)}, bf16[136,256]{1,0:T(8,128)(2,1)S(1)}, u32[]{:S(2)}, u32[]{:S(2)}) %collective-permute-start.3) | collective-permute-done | bytes 69664 | tf_op jit(solution)/shard_map/ppermute | solution.py:322
  24.1 3.4 %collective-permute-done.4.from_b = bf16[136,256]{1,0:T(8,128)(2,1)S(1)} collective-permute-done((bf16[136,256]{1,0:T(8,128)(2,1)}, bf16[136,256]{1,0:T(8,128)(2,1)S(1)}, u32[]{:S(2)}, u32[]{:S(2)}) %collective-permute-start.4) | collective-permute-done | bytes 69664 | tf_op jit(solution)/shard_map/ppermute | solution.py:322
  27.5 0.6 %copy-done.12 = bf16[136,256]{1,0:T(8,128)(2,1)} copy-done((bf16[136,256]{1,0:T(8,128)(2,1)}, bf16[136,256]{1,0:T(8,128)(2,1)S(1)}, u32[]{:S(2)}) %copy-start.12) | copy-done | bytes 69656
  28.1 0.0 all-to-all-done
  28.1 0.0 copy-done.14
  28.1 0.0 copy-done.15
  28.1 0.0 copy-done.17
  28.2 0.0 copy-done.1
  28.2 0.0 copy-done.2
  28.2 0.0 copy-done.3
  28.2 0.0 copy-done.4
  28.2 0.0 copy-done.5
  28.2 0.0 copy-start.6
  28.2 0.9 %copy-done.6 = bf16[256,256]{1,0:T(8,128)(2,1)S(1)} copy-done((bf16[256,256]{1,0:T(8,128)(2,1)S(1)}, bf16[256,256]{1,0:T(8,128)(2,1)}, u32[]{:S(2)}) %copy-start.6) | copy-done | bytes 131096
  29.1 0.9 %copy-done.7 = bf16[256,256]{1,0:T(8,128)(2,1)S(1)} copy-done((bf16[256,256]{1,0:T(8,128)(2,1)S(1)}, bf16[256,256]{1,0:T(8,128)(2,1)}, u32[]{:S(2)}) %copy-start.7) | copy-done | bytes 131096
  30.0 0.9 %copy-done.8 = bf16[256,256]{1,0:T(8,128)(2,1)S(1)} copy-done((bf16[256,256]{1,0:T(8,128)(2,1)S(1)}, bf16[256,256]{1,0:T(8,128)(2,1)}, u32[]{:S(2)}) %copy-start.8) | copy-done | bytes 131096
  30.9 0.9 %copy-done.13 = bf16[136,256]{1,0:T(8,128)(2,1)S(1)} copy-done((bf16[136,256]{1,0:T(8,128)(2,1)S(1)}, bf16[136,256]{1,0:T(8,128)(2,1)}, u32[]{:S(2)}) %copy-start.13) | copy-done | bytes 69656
  31.8 9.5 %shard_map.139 = bf16[512,256]{1,0:T(8,128)(2,1)} custom-call(s32[2]{0:T(128)S(1)} %pad_add_fusion.odd, f32[1,256]{1,0:T(1,128)S(1)} %reshape_reshape.3.scale, bf16[512,256]{1,0:T(8,128)(2,1)S(1)} %bitcast.8, f32[2,1600,128]{2,1,0:T(8,128)S(1)} %get-tuple-element.18.fine, f32[2,288,128]{2,1,0:T(8,128)S(1)} %get-tuple-element.19.mid, ...), custom_call_target="tpu_custom_call" | custom-call | tf_op jit(solution)/shard_map/pallas_call | solution.py:55
  (12 shorter events, 0.0 us)
Async XLA Ops:
  0.0 28.1 %copy-start.14 = (f32[16,256]{1,0:T(8,128)S(1)}, f32[16,256]{1,0:T(8,128)}, u32[]{:S(2)}) copy-start(f32[16,256]{1,0:T(8,128)} %constant.35.clone.fine_bias) | copy-start | bytes 49156
  0.0 28.1 %copy-start.15 = (f32[8,256]{1,0:T(8,128)S(1)}, f32[8,256]{1,0:T(8,128)}, u32[]{:S(2)}) copy-start(f32[8,256]{1,0:T(8,128)} %constant.36.clone.mid_bias) | copy-start | bytes 24580
  0.0 23.5 %copy-start.18 = (f32[8]{0:T(128)S(1)}, f32[8]{0:T(128)}, u32[]{:S(2)}) copy-start(f32[8]{0:T(128)} %param.19) | copy-start | bytes 100
  0.0 28.1 %copy-start.17 = (f32[256]{0:T(256)S(1)}, f32[256]{0:T(256)}, u32[]{:S(2)}) copy-start(f32[256]{0:T(256)} %param.21) | copy-start | bytes 3076
  0.1 0.9 %copy-start = (bf16[8,8,8,256]{3,2,1,0:T(8,128)(2,1)S(1)}, bf16[8,8,8,256]{3,2,1,0:T(8,128)(2,1)}, u32[]{:S(2)}) copy-start(bf16[8,8,8,256]{3,2,1,0:T(8,128)(2,1)} %param.14) | copy-start | bytes 786436
  1.0 0.9 %copy-start.11 = (bf16[80,512]{1,0:T(8,128)(2,1)S(1)}, bf16[80,512]{1,0:T(8,128)(2,1)}, u32[]{:S(2)}) copy-start(bf16[80,512]{1,0:T(8,128)(2,1)} %constant.34.clone.pool) | copy-start | bytes 245764
  1.9 0.7 %copy-start.16 = (f32[256]{0:T(256)S(1)}, f32[256]{0:T(256)}, u32[]{:S(2)}) copy-start(f32[256]{0:T(256)} %param.15) | copy-start | bytes 3076
  2.6 25.6 %copy-start.1 = (bf16[8,8,8,256]{3,2,1,0:T(8,128)(2,1)S(1)}, bf16[8,8,8,256]{3,2,1,0:T(8,128)(2,1)}, u32[]{:S(2)}) copy-start(bf16[8,8,8,256]{3,2,1,0:T(8,128)(2,1)} %param.14) | copy-start | bytes 786436
  2.6 25.6 %copy-start.2 = (bf16[256,512]{1,0:T(8,128)(2,1)S(1)}, bf16[256,512]{1,0:T(8,128)(2,1)}, u32[]{:S(2)}) copy-start(bf16[256,512]{1,0:T(8,128)(2,1)} %up_weight.1) | copy-start | bytes 786436
  2.6 25.6 %copy-start.3 = (bf16[512,256]{1,0:T(8,128)(2,1)S(1)}, bf16[512,256]{1,0:T(8,128)(2,1)}, u32[]{:S(2)}) copy-start(bf16[512,256]{1,0:T(8,128)(2,1)} %down_weight.1) | copy-start | bytes 786436
  2.6 25.6 %copy-start.4 = (bf16[256,256]{1,0:T(8,128)(2,1)S(1)}, bf16[256,256]{1,0:T(8,128)(2,1)}, u32[]{:S(2)}) copy-start(bf16[256,256]{1,0:T(8,128)(2,1)} %query_weight.1) | copy-start | bytes 393220
  2.6 25.6 %copy-start.5 = (bf16[256,256]{1,0:T(8,128)(2,1)S(1)}, bf16[256,256]{1,0:T(8,128)(2,1)}, u32[]{:S(2)}) copy-start(bf16[256,256]{1,0:T(8,128)(2,1)} %key_weight.1) | copy-start | bytes 393220
  3.6 3.2 %collective-permute-start = (bf16[80,256]{1,0:T(8,128)(2,1)S(1)}, bf16[80,256]{1,0:T(8,128)(2,1)S(1)}, u32[]{:S(2)}, u32[]{:S(2)}) collective-permute-start(bf16[80,256]{1,0:T(8,128)(2,1)S(1)} %get-tuple-element.16), channel_id=1, source_target_pairs={{0,8},{8,0},{16,24},{24,16},{1,9},{9,1},{17,25},{25,17},{2,10},{10... | collective-permute-start | bytes 122888 | tf_op jit(solution)/shard_map/ppermute | solution.py:322
  4.1 4.5 %collective-permute-start.1 = (bf16[80,256]{1,0:T(8,128)(2,1)S(1)}, bf16[80,256]{1,0:T(8,128)(2,1)S(1)}, u32[]{:S(2)}, u32[]{:S(2)}) collective-permute-start(bf16[80,256]{1,0:T(8,128)(2,1)S(1)} %get-tuple-element.17), channel_id=1, source_target_pairs={{8,16},{16,8},{24,0},{0,24},{9,17},{17,9},{25,1},{1,25},{10,18},{1... | collective-permute-start | bytes 122888 | tf_op jit(solution)/shard_map/ppermute | solution.py:322
  9.2 7.2 %collective-permute-start.2 = (bf16[208,256]{1,0:T(8,128)(2,1)S(1)}, bf16[208,256]{1,0:T(8,128)(2,1)S(1)}, u32[]{:S(2)}, u32[]{:S(2)}) collective-permute-start(bf16[208,256]{1,0:T(8,128)(2,1)S(1)} %shard_map.137), channel_id=1, source_target_pairs={{0,4},{4,0},{1,5},{5,1},{2,6},{6,2},{3,7},{7,3},{8,12},{12,8},{9,1... | collective-permute-start | bytes 319496 | tf_op jit(solution)/shard_map/ppermute | solution.py:322
  11.4 16.7 %all-to-all-start = ((bf16[32,8,256]{2,1,0:T(8,128)(2,1)}), bf16[32,8,256]{2,1,0:T(8,128)(2,1)S(1)}, u32[]{:S(2)}, u32[]{:S(2)}) async-start(bf16[32,8,256]{2,1,0:T(8,128)(2,1)} %broadcast_in_dim.10), calls=%async_computation | async-start | bytes 262144 | tf_op jit(solution)/shard_map/all_to_all | solution.py:399
  16.3 0.6 %copy-start.9 = (bf16[208,256]{1,0:T(8,128)(2,1)}, bf16[208,256]{1,0:T(8,128)(2,1)S(1)}, u32[]{:S(2)}) copy-start(bf16[208,256]{1,0:T(8,128)(2,1)S(1)} %collective-permute-done.2.refs_0_) | copy-start | bytes 319492
  17.0 0.9 %copy-start.10 = (bf16[208,256]{1,0:T(8,128)(2,1)S(1)}, bf16[208,256]{1,0:T(8,128)(2,1)}, u32[]{:S(2)}) copy-start(bf16[208,256]{1,0:T(8,128)(2,1)} %copy-done.9) | copy-start | bytes 319492
  19.3 4.8 %collective-permute-start.3 = (bf16[136,256]{1,0:T(8,128)(2,1)}, bf16[136,256]{1,0:T(8,128)(2,1)S(1)}, u32[]{:S(2)}, u32[]{:S(2)}) collective-permute-start(bf16[136,256]{1,0:T(8,128)(2,1)} %get-tuple-element.20), channel_id=1, source_target_pairs={{0,1},{1,0},{2,3},{3,2},{4,5},{5,4},{6,7},{7,6},{8,9},{9,8},{10,11... | collective-permute-start | bytes 208904 | tf_op jit(solution)/shard_map/ppermute | solution.py:322
  21.1 6.4 %collective-permute-start.4 = (bf16[136,256]{1,0:T(8,128)(2,1)}, bf16[136,256]{1,0:T(8,128)(2,1)S(1)}, u32[]{:S(2)}, u32[]{:S(2)}) collective-permute-start(bf16[136,256]{1,0:T(8,128)(2,1)} %get-tuple-element.21), channel_id=1, source_target_pairs={{1,2},{2,1},{3,0},{0,3},{5,6},{6,5},{7,4},{4,7},{9,10},{10,9},{11,... | collective-permute-start | bytes 208904 | tf_op jit(solution)/shard_map/ppermute | solution.py:322
  27.5 0.6 %copy-start.12 = (bf16[136,256]{1,0:T(8,128)(2,1)}, bf16[136,256]{1,0:T(8,128)(2,1)S(1)}, u32[]{:S(2)}) copy-start(bf16[136,256]{1,0:T(8,128)(2,1)S(1)} %collective-permute-done.4.from_b) | copy-start | bytes 208900
  28.2 0.9 %copy-start.6 = (bf16[256,256]{1,0:T(8,128)(2,1)S(1)}, bf16[256,256]{1,0:T(8,128)(2,1)}, u32[]{:S(2)}) copy-start(bf16[256,256]{1,0:T(8,128)(2,1)} %value_weight.1) | copy-start | bytes 393220
  29.1 0.9 %copy-start.7 = (bf16[256,256]{1,0:T(8,128)(2,1)S(1)}, bf16[256,256]{1,0:T(8,128)(2,1)}, u32[]{:S(2)}) copy-start(bf16[256,256]{1,0:T(8,128)(2,1)} %out_weight.1) | copy-start | bytes 393220
  30.0 0.9 %copy-start.8 = (bf16[256,256]{1,0:T(8,128)(2,1)S(1)}, bf16[256,256]{1,0:T(8,128)(2,1)}, u32[]{:S(2)}) copy-start(bf16[256,256]{1,0:T(8,128)(2,1)} %constant.37.clone.mask) | copy-start | bytes 393220
  30.9 0.9 %copy-start.13 = (bf16[136,256]{1,0:T(8,128)(2,1)S(1)}, bf16[136,256]{1,0:T(8,128)(2,1)}, u32[]{:S(2)}) copy-start(bf16[136,256]{1,0:T(8,128)(2,1)} %copy-done.12) | copy-start | bytes 208900
where the time goes:
time: 41.7 us; the launch traced here: 41.3 us
  starting transfers between devices  13.8 us (33%)
  Pallas kernels  12.5 us (30%)
  local copies, waits for them, and re-layouts  9.12 us (22%)
  waiting for transfers between devices  5.73 us (14%)
    pallas_call x4, Pallas kernels, call(): pl.pallas_call(kernel, out_shape=kinds, in_specs=[pl.BlockSpec(memory_spa...  12.5 us
    ppermute x5, starting transfers between devices, swap(): return lax.ppermute(array, axis, pairs)  8.89 us
    unnamed x38, local copies, waits for them, and re-layouts  8.29 us
    ppermute x5, waiting for transfers between devices, swap(): return lax.ppermute(array, axis, pairs)  5.72 us
    all_to_all x1, starting transfers between devices, shards(): lax.all_to_all(jnp.broadcast_to(coarse[None, :size.coarse], (nx * ny * nz...  4.92 us
  transfers between devices with their start and end apart: 6, of which 3 were waited for; matrix products, arithmetic and copies ran while one was open for 2% of the time, Pallas kernels for 4%

commit v1 on v0

v1 whole, which is shorter than its diff:
```python
import functools
import math

import jax
import jax.numpy as jnp
import numpy as np
from jax import lax
from jax.experimental import pallas as pl
from jax.experimental.pallas import tpu as pltpu
from jax.sharding import PartitionSpec as P

HEADS = 8
EPSILON = 1e-05
LOG2E = 1.4426950408889634
NEGATIVE = -1e30
LANES = 128
F32 = jnp.float32
BF16 = jnp.bfloat16
AXES = ("gx", "gy", "gz")


def up_to(count, step):
    return -(-count // step) * step


def layer_norm(values, gain):
    average = jnp.mean(values, axis=-1, keepdims=True)
    centered = values - average
    variance = jnp.mean(centered * centered, axis=-1, keepdims=True)
    return (centered * lax.rsqrt(variance + EPSILON) * gain).astype(BF16)


def dot(left, right):
    return jnp.dot(left, right, preferred_element_type=F32)


def dot_nt(left, right):
    return lax.dot_general(left, right, (((1,), (1,)), ((), ())), preferred_element_type=F32)


def dot_tn(left, right):
    return lax.dot_general(left, right, (((0,), (0,)), ((), ())), preferred_element_type=F32)


def joined(ref, rows):
    return jnp.concatenate([ref[j, rows, :] for j in range(ref.shape[0])], axis=1)


def split_store(ref, rows, values):
    for j in range(ref.shape[0]):
        ref[j, rows, :] = values[:, j * LANES : (j + 1) * LANES]


def call(kernel, outs, *args, spaces=None, scratch=(), vmem=True, aliases=None, limit=24 << 20, work=None):
    kinds = [pltpu.VMEM(s, d) if vmem else jax.ShapeDtypeStruct(s, d) for s, d in outs]
    spaces = spaces or [pltpu.VMEM] * len(args)
    return pl.pallas_call(
        kernel,
        out_shape=kinds,
        in_specs=[pl.BlockSpec(memory_space=s) for s in spaces],
        out_specs=[pl.BlockSpec(memory_space=pltpu.VMEM) for _ in outs],
        scratch_shapes=list(scratch),
        input_output_aliases=aliases or {},
        compiler_params=pltpu.CompilerParams(vmem_limit_bytes=limit),
        cost_estimate=work and pl.CostEstimate(flops=work, bytes_accessed=0, transcendentals=0),
    )(*args)


class Sizes:
    def __init__(self, extent, channels):
        self.x, self.y, self.z = extent
        self.c = channels
        self.parts = channels // LANES
        self.cells = self.x * self.y * self.z
        self.mx, self.my, self.mz = (n // 2 for n in extent)
        self.mids = self.mx * self.my * self.mz
        self.coarse = self.mids // 8
        self.mzp = up_to(self.mz + 2, 8)
        self.fine_rows = (self.x + 2) * (self.y + 2) * self.z
        self.mid_rows = (self.mx + 2) * (self.my + 2) * self.mzp
        self.fy, self.gy = self.x * self.z, self.mx * self.mz
        self.fx, self.gx = (self.y + 2) * self.z, (self.my + 2) * self.mz
        self.fz, self.gz = (self.x + 2) * (self.y + 2), (self.mx + 2) * (self.my + 2)
        self.fzp, self.gzp = up_to(self.fz, 8), up_to(self.gz, 8)
        self.groups = [(bx, by) for bx in range(self.x // 2) for by in range(self.y // 2)]
        self.group = 4 * self.z

    def query_rows(self, bx, by):
        return [
            slice(((2 * bx + dx) * self.y + 2 * by) * self.z, ((2 * bx + dx) * self.y + 2 * by + 2) * self.z)
            for dx in (0, 1)
        ]


def pooling(size):
    x, y, z = np.unravel_index(np.arange(size.cells), (size.x, size.y, size.z))
    middle = ((x // 2) * size.my + y // 2) * size.mz + z // 2
    coarse = ((x // 4) * (size.my // 2) + y // 4) * (size.mz // 2) + z // 4
    rows = np.zeros((size.mids + size.coarse, size.cells), np.float32)
    rows[middle, np.arange(size.cells)] = 1.0
    rows[size.mids + coarse, np.arange(size.cells)] = 1.0
    grid = rows[: size.mids].reshape(size.mx, size.my, size.mz, size.cells)
    faces = [grid[:, at].reshape(size.gy, size.cells) for at in (0, size.my - 1)]
    return np.concatenate([rows, rows[size.mids :], *faces]).astype(jnp.bfloat16)


def window_bias(size):
    query_z = np.arange(size.group) % size.z

    def seen(keys, factor):
        start = 2 * (query_z // factor)
        return (keys[:, None] >= start - 1) & (keys[:, None] <= start + 2)

    place = np.arange(size.mzp)
    middle = np.where(place < size.mz, place, np.where(place == size.mz, -1, size.mz))
    held = seen(middle, 4) & (place[:, None] < size.mz + 2)
    rows = np.concatenate([seen(np.arange(size.z), 2), held, seen(np.array([-1, size.z]), 2)])
    bias = np.where(rows, 0.0, NEGATIVE).astype(np.float32)
    bias = np.concatenate([bias, np.zeros((up_to(len(bias), 8) - len(bias), size.group), np.float32)])
    return np.tile(bias, (1, HEADS))


def arranging(size):
    rows = np.zeros((len(size.groups) * 32, 2 * size.fzp), np.float32)
    at = 0
    for bx, by in size.groups:
        for side in range(2):
            for kx in range(4):
                for ky in range(4):
                    rows[at, side * size.fzp + (2 * bx + kx) * (size.y + 2) + 2 * by + ky] = 1.0
                    at += 1
    return rows.astype(jnp.bfloat16)


def head_mask(size):
    head = np.arange(HEADS * size.group) // size.group
    return (head[:, None] == np.arange(size.c)[None, :] // (size.c // HEADS)).astype(jnp.bfloat16)


def fetch(sources, targets, sems):
    copies = [pltpu.make_async_copy(s, t, sems.at[i]) for i, (s, t) in enumerate(zip(sources, targets))]
    for copy in copies:
        copy.start()
    return copies


def is_odd(axis):
    return lax.axis_index(axis) % 2 == 1


def first_kernel(size, devices, tokens, gain, pool, both, faces, coarse_out, cells, gain_here, pool_here, sems):
    copies = fetch((tokens, gain, pool), (cells, gain_here, pool_here), sems)
    for copy in copies[:2]:
        copy.wait()
    values = layer_norm(cells[...].astype(F32), gain_here[...])
    both[: size.cells, :] = values
    copies[2].wait()
    pooled = dot(pool_here[...], values)
    at = size.mids + 2 * size.coarse
    both[size.cells :, :] = (pooled[: size.mids] * 0.125).astype(BF16)
    pack = (pooled[size.mids : at] * (1.0 / 64.0)).astype(BF16)
    for row in range(0, devices * size.coarse, 2 * size.coarse):
        coarse_out[row : row + 2 * size.coarse, :] = pack
    face = size.fy + size.gy
    for side, y in enumerate((0, size.y - 1)):
        rows = [slice((x * size.y + y) * size.z, (x * size.y + y + 1) * size.z) for x in range(size.x)]
        cut = jnp.concatenate([values[r].astype(F32) for r in rows], axis=0)
        faces[side * face : side * face + size.fy, :] = cut.astype(BF16)
        mids = pooled[at + side * size.gy : at + (side + 1) * size.gy] * 0.125
        faces[side * face + size.fy : (side + 1) * face, :] = mids.astype(BF16)


def prepare_kernel(size, both, after, *refs):
    held = (len(refs) - 4) // 2
    sources, targets = refs[:held], refs[held : 2 * held]
    queries, fine, mid, sems = refs[2 * held :]
    copies = fetch(sources, targets, sems)
    cells = both[: size.cells, :].astype(F32)
    mids = both[size.cells :, :].astype(F32)
    mid[...] = jnp.zeros_like(mid)
    for x in range(size.x):
        at = ((x + 1) * (size.y + 2) + 1) * size.z
        split_store(fine, slice(at, at + size.y * size.z), cells[x * size.y * size.z : (x + 1) * size.y * size.z])
    for x in range(size.mx):
        for y in range(size.my):
            at = ((x + 1) * (size.my + 2) + y + 1) * size.mzp
            row = (x * size.my + y) * size.mz
            split_store(mid, slice(at, at + size.mz), mids[row : row + size.mz])
    copies[0].wait()
    queries[...] = dot(both[: size.cells, :], targets[0][...]).astype(BF16)
    for copy in copies[1:]:
        copy.wait()


def pick(odd, from_a, from_b):
    first, second = from_a[...].astype(F32), from_b[...].astype(F32)
    return jnp.where(odd, first, second), jnp.where(odd, second, first)


def from_sides(size, y_refs):
    if len(y_refs) == 1:
        both = y_refs[0][...].astype(F32)
        return both[size.fy + size.gy :], both[: size.fy + size.gy]
    return y_refs[0][...].astype(F32), y_refs[1][...].astype(F32)


def x_kernel(size, both, *refs):
    y_refs, (face_a, face_b) = refs[:-2], refs[-2:]
    y_low, y_high = from_sides(size, y_refs)
    cells = both[: size.cells, :].astype(F32)
    mids = both[size.cells :, :].astype(F32)

    def cut(x, mx):
        fine_at, own = slice(x * size.z, (x + 1) * size.z), size.y * size.z
        mid_at, own_mid = slice(size.fy + mx * size.mz, size.fy + (mx + 1) * size.mz), size.my * size.mz
        return jnp.concatenate(
            [
                y_low[fine_at],
                cells[x * own : (x + 1) * own],
                y_high[fine_at],
                y_low[mid_at],
                mids[mx * own_mid : (mx + 1) * own_mid],
                y_high[mid_at],
            ],
            axis=0,
        )

    low, high = cut(0, 0), cut(size.x - 1, size.mx - 1)
    odd = is_odd("gx")
    face_a[...] = jnp.where(odd, low, high).astype(BF16)
    face_b[...] = jnp.where(odd, high, low).astype(BF16)


def z_kernel(size, fine_in, mid_in, from_a, from_b, *refs):
    y_refs, (face_a, face_b, fine, mid) = refs[:-4], refs[-4:]
    y_low, y_high = from_sides(size, y_refs)
    low, high = pick(is_odd("gx"), from_a, from_b)
    for x, halo in ((0, low), (size.x + 1, high)):
        split_store(fine, slice(x * size.fx, (x + 1) * size.fx), halo[: size.fx])
    for x, halo in ((0, low), (size.mx + 1, high)):
        for y in range(size.my + 2):
            at = (x * (size.my + 2) + y) * size.mzp
            row = size.fx + y * size.mz
            split_store(mid, slice(at, at + size.mz), halo[row : row + size.mz])
    for y, my, halo in ((0, 0, y_low), (size.y + 1, size.my + 1, y_high)):
        for x in range(size.x):
            at = ((x + 1) * (size.y + 2) + y) * size.z
            split_store(fine, slice(at, at + size.z), halo[x * size.z : (x + 1) * size.z])
        for x in range(size.mx):
            at = ((x + 1) * (size.my + 2) + my) * size.mzp
            row = size.fy + x * size.mz
            split_store(mid, slice(at, at + size.mz), halo[row : row + size.mz])

    def cut(z, mz):
        parts = [
            joined(fine, pl.ds(z, size.fz, stride=size.z)),
            jnp.zeros((size.fzp - size.fz, size.c), F32),
            joined(mid, pl.ds(mz, size.gz, stride=size.mzp)),
            jnp.zeros((size.gzp - size.gz, size.c), F32),
        ]
        return jnp.concatenate([p for p in parts if p.shape[0]], axis=0)

    below, above = cut(0, 0), cut(size.z - 1, size.mz - 1)
    odd = is_odd("gz")
    face_a[...] = jnp.where(odd, below, above).astype(BF16)
    face_b[...] = jnp.where(odd, above, below).astype(BF16)


def lane_scale(size, head_scale):
    factor = LOG2E / math.sqrt(size.c // HEADS)
    return jnp.concatenate([jnp.full((1, size.group), head_scale[h] * factor, F32) for h in range(HEADS)], axis=1)


def spread_queries(size, queries, rows, mask):
    some = jnp.concatenate([queries[r, :] for r in rows], axis=0)
    return jnp.concatenate([some] * HEADS, axis=0) * mask


def soft(scores):
    weights = jnp.exp2(scores - jnp.max(scores, axis=0, keepdims=True))
    return (weights * (1.0 / jnp.sum(weights, axis=0, keepdims=True))).astype(BF16)


def gather_heads(size, total, wide):
    return jnp.sum(total.reshape(HEADS, size.group, size.c) * wide, axis=0)


def coarse_kernel(
    size, head_scale, queries, fine, coarse, key_weight, value_weight, mask, coarse_out, keys, values, scale_here, sems
):
    copy = fetch((head_scale,), (scale_here,), sems)[0]
    block = joined(fine, slice(None)).astype(BF16)
    keys[...] = dot(block, key_weight[...]).astype(BF16)
    values[...] = dot(block, value_weight[...]).astype(BF16)
    cells = coarse[...]
    coarse_keys = dot(cells, key_weight[...]).astype(BF16)
    coarse_values = dot(cells, value_weight[...]).astype(BF16)
    copy.wait()
    scale = lane_scale(size, scale_here)
    spread_mask = mask[...]
    wide = spread_mask.astype(F32).reshape(HEADS, size.group, size.c)
    for bx, by in size.groups:
        rows = size.query_rows(bx, by)
        spread = spread_queries(size, queries, rows, spread_mask)
        total = dot_tn(soft(dot_nt(coarse_keys, spread) * scale), coarse_values)
        result = gather_heads(size, total, wide)
        for k, r in enumerate(rows):
            coarse_out[r, :] = result[k * 2 * size.z : (k + 1) * 2 * size.z]


def last_kernel(
    size,
    head_scale,
    tokens,
    mlp_gain,
    biases,
    queries,
    keys,
    values,
    mid_in,
    from_a,
    from_b,
    coarse_out,
    key_weight,
    value_weight,
    out_weight,
    up_weight,
    down_weight,
    mask,
    arrange,
    out,
    mid,
    attended,
    scale_here,
    tokens_here,
    gain_here,
    bias,
    sems,
):
    copies = fetch((biases, head_scale, tokens, mlp_gain), (bias, scale_here, tokens_here, gain_here), sems)
    low, high = pick(is_odd("gz"), from_a, from_b)
    mid[...] = mid_in[...]
    split_store(mid, pl.ds(size.mz, size.gz, stride=size.mzp), low[size.fzp : size.fzp + size.gz])
    split_store(mid, pl.ds(size.mz + 1, size.gz, stride=size.mzp), high[size.fzp : size.fzp + size.gz])
    ends = jnp.concatenate([low[: size.fzp], high[: size.fzp]], axis=0).astype(BF16)
    ends = dot(arrange[...], ends).astype(BF16)
    end_keys = dot(ends, key_weight[...]).astype(BF16)
    end_values = dot(ends, value_weight[...]).astype(BF16)
    mids = joined(mid, slice(None)).astype(BF16)
    mid_keys = dot(mids, key_weight[...]).astype(BF16)
    mid_values = dot(mids, value_weight[...]).astype(BF16)

    for copy in copies:
        copy.wait()
    scale = lane_scale(size, scale_here)
    spread_mask = mask[...]
    wide = spread_mask.astype(F32).reshape(HEADS, size.group, size.c)
    run_bias = bias[: size.z]
    mid_bias = bias[size.z : size.z + size.mzp]
    low_bias = bias[size.z + size.mzp : size.z + size.mzp + 1]
    high_bias = bias[size.z + size.mzp + 1 : size.z + size.mzp + 2]
    fine_row = (size.y + 2) * size.z
    mid_row = (size.my + 2) * size.mzp

    def tiled(scores, one):
        length = one.shape[0]
        return (scores.reshape(-1, length, scores.shape[-1]) + one[None]).reshape(scores.shape)

    for index, (bx, by) in enumerate(size.groups):
        rows = size.query_rows(bx, by)
        spread = spread_queries(size, queries, rows, spread_mask)
        slabs = [
            slice((2 * bx + k) * fine_row + 2 * by * size.z, (2 * bx + k) * fine_row + (2 * by + 4) * size.z)
            for k in range(4)
        ]
        ends_at = slice(32 * index, 32 * index + 32)
        some_keys = jnp.concatenate([keys[s, :] for s in slabs] + [end_keys[ends_at]], axis=0)
        some_values = jnp.concatenate([values[s, :] for s in slabs] + [end_values[ends_at]], axis=0)
        scores = dot_nt(some_keys, spread) * scale
        inner = 16 * size.z
        scores = jnp.concatenate(
            [
                tiled(scores[:inner], run_bias),
                scores[inner : inner + 16] + low_bias,
                scores[inner + 16 :] + high_bias,
            ],
            axis=0,
        )
        total = dot_tn(soft(scores), some_values)
        slabs = [
            slice(
                (2 * (bx // 2) + k) * mid_row + 2 * (by // 2) * size.mzp,
                (2 * (bx // 2) + k) * mid_row + (2 * (by // 2) + 4) * size.mzp,
            )
            for k in range(4)
        ]
        some_keys = jnp.concatenate([mid_keys[s] for s in slabs], axis=0)
        some_values = jnp.concatenate([mid_values[s] for s in slabs], axis=0)
        scores = tiled(dot_nt(some_keys, spread) * scale, mid_bias)
        total = total + dot_tn(soft(scores), some_values)
        result = gather_heads(size, total, wide)
        for k, r in enumerate(rows):
            part = result[k * 2 * size.z : (k + 1) * 2 * size.z]
            attended[r, :] = (part + coarse_out[r, :]).astype(BF16)

    residual = (tokens_here[...].astype(F32) + dot(attended[...], out_weight[...])).astype(BF16)
    second = layer_norm(residual.astype(F32), gain_here[...])
    hidden = jax.nn.gelu(dot(second, up_weight[...]), approximate=True).astype(BF16)
    out[...] = (residual.astype(F32) + dot(hidden, down_weight[...])).astype(BF16)


def swap(array, axis, start):
    count = lax.axis_size(axis)
    pairs = []
    for i in range(start, count, 2):
        other = (i + 1) % count
        pairs += [(i, other), (other, i)]
    return lax.ppermute(array, axis, pairs)


def shift(array, axis, by):
    count = lax.axis_size(axis)
    return lax.ppermute(array, axis, [(i, (i + by) % count) for i in range(count)])


def shards(
    tokens,
    norm_gain,
    query_weight,
    key_weight,
    value_weight,
    head_scale,
    out_weight,
    mlp_gain,
    up_weight,
    down_weight,
):
    channels = tokens.shape[-1]
    size = Sizes(tokens.shape[:3], channels)
    devices = math.prod(lax.axis_size(a) for a in AXES)
    fx, gx, fy, gy = size.fx, size.gx, size.fy, size.gy
    face_z = size.fzp + size.gzp
    smem, vmem, hbm = pltpu.SMEM, pltpu.VMEM, pltpu.HBM

    def pinned(*arrays):
        return [pltpu.with_memory_space_constraint(jnp.asarray(a), hbm) for a in arrays]

    flat, gain, gain_mlp, scales = pinned(
        tokens.reshape(size.cells, channels), norm_gain.reshape(1, -1), mlp_gain.reshape(1, -1), head_scale
    )
    biases, pool = pinned(window_bias(size), pooling(size))
    both, faces, coarse = call(
        functools.partial(first_kernel, size, devices),
        [
            ((size.cells + size.mids, channels), BF16),
            ((2 * (fy + gy), channels), BF16),
            ((devices * size.coarse, channels), BF16),
        ],
        flat,
        gain,
        pool,
        spaces=[hbm] * 3,
        scratch=[
            pltpu.VMEM(flat.shape, BF16),
            pltpu.VMEM(gain.shape, F32),
            pltpu.VMEM(pool.shape, BF16),
            pltpu.SemaphoreType.DMA((3,)),
        ],
    )
    if lax.axis_size("gy") == 2:
        from_y = [swap(faces, "gy", 0)]
    else:
        from_y = [shift(faces[fy + gy :], "gy", 1), shift(faces[: fy + gy], "gy", -1)]
    gathered = lax.all_to_all(coarse.reshape(devices, size.coarse, channels), AXES, 0, 0).reshape(-1, channels)
    face_a, face_b = call(
        functools.partial(x_kernel, size),
        [((fx + gx, channels), BF16), ((fx + gx, channels), BF16)],
        both,
        *from_y,
        work=20_000_000_000,
    )
    from_a = swap(face_a, "gx", 0)
    from_b = swap(face_b, "gx", 1)
    held = pinned(
        query_weight,
        key_weight,
        value_weight,
        head_mask(size),
        arranging(size),
        out_weight,
        up_weight,
        down_weight,
    )
    *weights, queries, fine, mid = call(
        functools.partial(prepare_kernel, size),
        [(a.shape, a.dtype) for a in held]
        + [
            ((size.cells, channels), BF16),
            ((size.parts, size.fine_rows, LANES), F32),
            ((size.parts, size.mid_rows, LANES), F32),
        ],
        both,
        face_a,
        *held,
        spaces=[vmem] * 2 + [hbm] * len(held),
        scratch=[pltpu.SemaphoreType.DMA((len(held),))],
    )
    wq, wk, wv, mask, arrange, wo, wu, wd = weights
    z_a, z_b, fine, mid = call(
        functools.partial(z_kernel, size),
        [
            ((face_z, channels), BF16),
            ((face_z, channels), BF16),
            ((size.parts, size.fine_rows, LANES), F32),
            ((size.parts, size.mid_rows, LANES), F32),
        ],
        fine,
        mid,
        from_a,
        from_b,
        *from_y,
        aliases={0: 2, 1: 3},
    )
    got_a = swap(z_a, "gz", 0)
    got_b = swap(z_b, "gz", 1)
    coarse_out, keys, values = call(
        functools.partial(coarse_kernel, size),
        [
            ((size.cells, channels), F32),
            ((size.fine_rows, channels), BF16),
            ((size.fine_rows, channels), BF16),
        ],
        scales,
        queries,
        fine,
        gathered,
        wk,
        wv,
        mask,
        spaces=[hbm] + [vmem] * 6,
        scratch=[pltpu.SMEM((HEADS,), F32), pltpu.SemaphoreType.DMA((1,))],
    )
    out = call(
        functools.partial(last_kernel, size),
        [((size.cells, channels), BF16)],
        scales,
        flat,
        gain_mlp,
        biases,
        queries,
        keys,
        values,
        mid,
        got_a,
        got_b,
        coarse_out,
        wk,
        wv,
        wo,
        wu,
        wd,
        mask,
        arrange,
        spaces=[hbm] * 4 + [vmem] * 14,
        scratch=[
            pltpu.VMEM((size.parts, size.mid_rows, LANES), F32),
            pltpu.VMEM((size.cells, channels), BF16),
            pltpu.SMEM((HEADS,), F32),
            pltpu.VMEM(flat.shape, BF16),
            pltpu.VMEM(gain_mlp.shape, F32),
            pltpu.VMEM(biases.shape, F32),
            pltpu.SemaphoreType.DMA((4,)),
        ],
        vmem=False,
    )[0]
    return out.reshape(tokens.shape)


def solution(mesh):
    in_specs = (P("gx", "gy", "gz", None), P(), P(), P(), P(), P(), P(), P(), P(), P())
    out_specs = P("gx", "gy", "gz", None)
    return jax.shard_map(shards, mesh=mesh, in_specs=in_specs, out_specs=out_specs, check_vma=False)
```

time: 41.7 us -> 29.3 us (0.70)
  local copies, waits for them, and re-layouts: 9.12 us -> 0 us
  waiting for transfers between devices: 5.73 us -> 1.67 us
  starting transfers between devices: 13.8 us -> 14.7 us
    unnamed x38 -> x0, local copies, waits for them, and re-layouts: 8.29 us -> none
    ppermute x5, waiting for transfers between devices: 5.72 us -> 1.66 us  [swap(): return lax.ppermute(array, axis, pairs)]
    ppermute x5, starting transfers between devices: 8.89 us -> 9.82 us  [swap(): return lax.ppermute(array, axis, pairs)]
    broadcast_in_dim x2 -> x0, local copies, waits for them, and re-layouts: 0.74 us -> none  [the longest x1 0.67 us: shards(): jnp.broadcast_to(coarse[None, :size.coarse], (nx * ny * nz, size.coarse,...]
    pallas_call x4 -> x6, Pallas kernels: 12.5 us -> 12.6 us  [call(): pl.pallas_call(kernel, out_shape=kinds, in_specs=[pl.BlockSpec(memory_spa...]
  transfers between devices with their start and end apart: 6 -> 6, of which waited for: 3 -> 2; matrix products, arithmetic and copies ran while one was open for 2% -> 0% of each run, Pallas kernels for 4% -> 17%
where the time goes in v1:
time: 29.3 us; the launch traced here: 29.1 us
  starting transfers between devices  14.7 us (50%)
  Pallas kernels  12.6 us (43%)
  waiting for transfers between devices  1.67 us (6%)
    pallas_call x6, Pallas kernels, call(): pl.pallas_call(kernel, out_shape=kinds, in_specs=[pl.BlockSpec(memory_spa...  12.6 us
    ppermute x5, starting transfers between devices, swap(): return lax.ppermute(array, axis, pairs)  9.82 us
    all_to_all x1, starting transfers between devices, shards(): lax.all_to_all(coarse.reshape(devices, size.coarse, channels), AXES, 0, 0)  4.92 us
    ppermute x5, waiting for transfers between devices, swap(): return lax.ppermute(array, axis, pairs)  1.66 us
  transfers between devices with their start and end apart: 6, of which 2 were waited for; matrix products, arithmetic and copies ran while one was open for 0% of the time, Pallas kernels for 17%

profile of v1, /device:TPU:0, one launch (start us, length us, event | category | flops | bytes accessed | tf_op | source)
XLA Modules:
  0.0 29.1 jit_solution(8149365572406918631)
XLA Ops:
  0.0 2.1 %shard_map.136 = (bf16[576,256]{1,0:T(8,128)(2,1)S(1)}, bf16[160,256]{1,0:T(8,128)(2,1)S(1)}, bf16[256,256]{1,0:T(8,128)(2,1)}) custom-call(bf16[512,256]{1,0:T(8,128)(2,1)} %bitcast.7, f32[1,256]{1,0:T(1,128)} %bitcast.9, bf16[112,512]{1,0:T(8,128)(2,1)} %constant.9.clone.pool), custom_call_target="tpu_custom_call" | custom-call | tf_op jit(solution)/shard_map/pallas_call | solution.py:57
  2.1 3.0 %collective-permute-start = (bf16[160,256]{1,0:T(8,128)(2,1)S(1)}, bf16[160,256]{1,0:T(8,128)(2,1)S(1)}, u32[]{:S(2)}, u32[]{:S(2)}) collective-permute-start(bf16[160,256]{1,0:T(8,128)(2,1)S(1)} %get-tuple-element.28), channel_id=1, source_target_pairs={{0,4},{4,0},{1,5},{5,1},{2,6},{6,2},{3,7},{7,3},{8,12},{12,8},{9,1... | collective-permute-start | bytes 245768 | tf_op jit(solution)/shard_map/ppermute | solution.py:418
  5.1 4.9 %all-to-all-start = ((bf16[32,8,256]{2,1,0:T(8,128)(2,1)}), bf16[32,8,256]{2,1,0:T(8,128)(2,1)S(1)}, u32[]{:S(2)}, u32[]{:S(2)}) async-start(bf16[32,8,256]{2,1,0:T(8,128)(2,1)} %bitcast.3), calls=%async_computation | async-start | bytes 262144 | tf_op jit(solution)/shard_map/all_to_all | solution.py:474
  10.0 0.0 collective-permute-done.refs_0_
  10.1 1.6 %collective-permute-start.2 = (bf16[104,256]{1,0:T(8,128)(2,1)S(1)}, bf16[104,256]{1,0:T(8,128)(2,1)S(1)}, u32[]{:S(2)}, u32[]{:S(2)}) collective-permute-start(bf16[104,256]{1,0:T(8,128)(2,1)S(1)} %get-tuple-element.33), channel_id=1, source_target_pairs={{8,16},{16,8},{24,0},{0,24},{9,17},{17,9},{25,1},{1,25},{10,18},{1... | collective-permute-start | bytes 159752 | tf_op jit(solution)/shard_map/ppermute | solution.py:418
  11.6 0.4 %collective-permute-start.1 = (bf16[104,256]{1,0:T(8,128)(2,1)S(1)}, bf16[104,256]{1,0:T(8,128)(2,1)S(1)}, u32[]{:S(2)}, u32[]{:S(2)}) collective-permute-start(bf16[104,256]{1,0:T(8,128)(2,1)S(1)} %get-tuple-element.29.after), channel_id=1, source_target_pairs={{0,8},{8,0},{16,24},{24,16},{1,9},{9,1},{17,25},{25,17},{2,10},{10... | collective-permute-start | bytes 159752 | tf_op jit(solution)/shard_map/ppermute | solution.py:418
  12.0 2.1 %shard_map.138 = (bf16[256,256]{1,0:T(8,128)(2,1)}, bf16[256,256]{1,0:T(8,128)(2,1)S(1)}, bf16[256,256]{1,0:T(8,128)(2,1)S(1)}, bf16[256,256]{1,0:T(8,128)(2,1)S...) custom-call(bf16[576,256]{1,0:T(8,128)(2,1)S(1)} %get-tuple-element., ...), custom_call_target="tpu_custom_call" | custom-call | tf_op jit(solution)/shard_map/pallas_call | solution.py:57
  14.1 0.1 collective-permute-done.2.from_b
  14.2 0.0 collective-permute-done.1.from_a
  14.2 0.1 shard_map.139
  14.3 2.1 %collective-permute-start.3 = (bf16[144,256]{1,0:T(8,128)(2,1)S(1)}, bf16[144,256]{1,0:T(8,128)(2,1)S(1)}, u32[]{:S(2)}, u32[]{:S(2)}) collective-permute-start(bf16[144,256]{1,0:T(8,128)(2,1)S(1)} %get-tuple-element.42), channel_id=1, source_target_pairs={{0,1},{1,0},{2,3},{3,2},{4,5},{5,4},{6,7},{7,6},{8,9},{9,8},{10,11... | collective-permute-start | bytes 221192 | tf_op jit(solution)/shard_map/ppermute | solution.py:418
  16.4 2.8 %collective-permute-start.4 = (bf16[144,256]{1,0:T(8,128)(2,1)S(1)}, bf16[144,256]{1,0:T(8,128)(2,1)S(1)}, u32[]{:S(2)}, u32[]{:S(2)}) collective-permute-start(bf16[144,256]{1,0:T(8,128)(2,1)S(1)} %get-tuple-element.43), channel_id=1, source_target_pairs={{1,2},{2,1},{3,0},{0,3},{5,6},{6,5},{7,4},{4,7},{9,10},{10,9},{11,... | collective-permute-start | bytes 221192 | tf_op jit(solution)/shard_map/ppermute | solution.py:418
  19.2 0.0 all-to-all-done
  19.2 2.6 %shard_map.140 = (f32[512,256]{1,0:T(8,128)S(1)}, bf16[800,256]{1,0:T(8,128)(2,1)S(1)}, bf16[800,256]{1,0:T(8,128)(2,1)S(1)}) custom-call(f32[8]{0:T(128)} %head_scale.3, bf16[512,256]{1,0:T(8,128)(2,1)S(1)} %get-tuple-element.30.queries, f32[2,800,128]{2,1,0:T(8,128)S(1)} %get-tuple-element.34.fine, bf16[256,256]{1,0:T(8,128)(2,1)S(1)} %bitcast.6, ...), custom_call_target="tpu_custom_call" | custom-call | tf_op jit(solution)/shard_map/pallas_call | solution.py:57
  21.8 0.0 collective-permute-done.3.from_a
  21.8 1.6 %collective-permute-done.4.from_b = bf16[144,256]{1,0:T(8,128)(2,1)S(1)} collective-permute-done((bf16[144,256]{1,0:T(8,128)(2,1)S(1)}, bf16[144,256]{1,0:T(8,128)(2,1)S(1)}, u32[]{:S(2)}, u32[]{:S(2)}) %collective-permute-start.4) | collective-permute-done | bytes 73760 | tf_op jit(solution)/shard_map/ppermute | solution.py:418
  23.4 5.7 %shard_map.141 = bf16[512,256]{1,0:T(8,128)(2,1)} custom-call(f32[8]{0:T(128)} %head_scale.3, bf16[512,256]{1,0:T(8,128)(2,1)} %bitcast.8, f32[1,256]{1,0:T(1,128)} %bitcast.10, f32[24,256]{1,0:T(8,128)} %constant.8.clone.biases, bf16[512,256]{1,0:T(8,128)(2,1)S(1)} %get-tuple-element.30.queries, bf16[800,256]{1,0:T(8,128)(2,1)S(1)} %get-tuple-element.39.keys, ...), custom_call_target="tpu_custom_call" | custom-call | tf_op jit(solution)/shard_map/pallas_call | solution.py:57
  (1 shorter events, 0.0 us)
Async XLA Ops:
  2.1 7.9 %collective-permute-start = (bf16[160,256]{1,0:T(8,128)(2,1)S(1)}, bf16[160,256]{1,0:T(8,128)(2,1)S(1)}, u32[]{:S(2)}, u32[]{:S(2)}) collective-permute-start(bf16[160,256]{1,0:T(8,128)(2,1)S(1)} %get-tuple-element.28), channel_id=1, source_target_pairs={{0,4},{4,0},{1,5},{5,1},{2,6},{6,2},{3,7},{7,3},{8,12},{12,8},{9,1... | collective-permute-start | bytes 245768 | tf_op jit(solution)/shard_map/ppermute | solution.py:418
  5.1 14.1 %all-to-all-start = ((bf16[32,8,256]{2,1,0:T(8,128)(2,1)}), bf16[32,8,256]{2,1,0:T(8,128)(2,1)S(1)}, u32[]{:S(2)}, u32[]{:S(2)}) async-start(bf16[32,8,256]{2,1,0:T(8,128)(2,1)} %bitcast.3), calls=%async_computation | async-start | bytes 262144 | tf_op jit(solution)/shard_map/all_to_all | solution.py:474
  10.1 4.1 %collective-permute-start.2 = (bf16[104,256]{1,0:T(8,128)(2,1)S(1)}, bf16[104,256]{1,0:T(8,128)(2,1)S(1)}, u32[]{:S(2)}, u32[]{:S(2)}) collective-permute-start(bf16[104,256]{1,0:T(8,128)(2,1)S(1)} %get-tuple-element.33), channel_id=1, source_target_pairs={{8,16},{16,8},{24,0},{0,24},{9,17},{17,9},{25,1},{1,25},{10,18},{1... | collective-permute-start | bytes 159752 | tf_op jit(solution)/shard_map/ppermute | solution.py:418
  11.6 2.6 %collective-permute-start.1 = (bf16[104,256]{1,0:T(8,128)(2,1)S(1)}, bf16[104,256]{1,0:T(8,128)(2,1)S(1)}, u32[]{:S(2)}, u32[]{:S(2)}) collective-permute-start(bf16[104,256]{1,0:T(8,128)(2,1)S(1)} %get-tuple-element.29.after), channel_id=1, source_target_pairs={{0,8},{8,0},{16,24},{24,16},{1,9},{9,1},{17,25},{25,17},{2,10},{10... | collective-permute-start | bytes 159752 | tf_op jit(solution)/shard_map/ppermute | solution.py:418
  14.3 7.5 %collective-permute-start.3 = (bf16[144,256]{1,0:T(8,128)(2,1)S(1)}, bf16[144,256]{1,0:T(8,128)(2,1)S(1)}, u32[]{:S(2)}, u32[]{:S(2)}) collective-permute-start(bf16[144,256]{1,0:T(8,128)(2,1)S(1)} %get-tuple-element.42), channel_id=1, source_target_pairs={{0,1},{1,0},{2,3},{3,2},{4,5},{5,4},{6,7},{7,6},{8,9},{9,8},{10,11... | collective-permute-start | bytes 221192 | tf_op jit(solution)/shard_map/ppermute | solution.py:418
  16.4 7.0 %collective-permute-start.4 = (bf16[144,256]{1,0:T(8,128)(2,1)S(1)}, bf16[144,256]{1,0:T(8,128)(2,1)S(1)}, u32[]{:S(2)}, u32[]{:S(2)}) collective-permute-start(bf16[144,256]{1,0:T(8,128)(2,1)S(1)} %get-tuple-element.43), channel_id=1, source_target_pairs={{1,2},{2,1},{3,0},{0,3},{5,6},{6,5},{7,4},{4,7},{9,10},{10,9},{11,... | collective-permute-start | bytes 221192 | tf_op jit(solution)/shard_map/ppermute | solution.py:418

commit v2 on v1

--- a/solution.py
+++ b/solution.py
@@ -78,6 +78,10 @@
         self.mzp = up_to(self.mz + 2, 8)
         self.fine_rows = (self.x + 2) * (self.y + 2) * self.z
         self.mid_rows = (self.mx + 2) * (self.my + 2) * self.mzp
+        self.bias_rows = up_to(self.z + self.mzp + 2, 8)
+        self.ones_at = self.mid_rows + self.bias_rows
+        self.scale_at = self.ones_at + 4 * self.z
+        self.kept_rows = self.scale_at + 8
         self.fy, self.gy = self.x * self.z, self.mx * self.mz
         self.fx, self.gx = (self.y + 2) * self.z, (self.my + 2) * self.mz
         self.fz, self.gz = (self.x + 2) * (self.y + 2), (self.mx + 2) * (self.my + 2)
@@ -117,7 +121,8 @@
     rows = np.concatenate([seen(np.arange(size.z), 2), held, seen(np.array([-1, size.z]), 2)])
     bias = np.where(rows, 0.0, NEGATIVE).astype(np.float32)
     bias = np.concatenate([bias, np.zeros((up_to(len(bias), 8) - len(bias), size.group), np.float32)])
-    return np.tile(bias, (1, HEADS))
+    rows = np.tile(np.concatenate([bias, np.eye(size.group, dtype=np.float32)]), (1, HEADS))
+    return np.ascontiguousarray(rows.reshape(len(rows), -1, LANES).transpose(1, 0, 2))
 
 
 def arranging(size):
@@ -170,14 +175,15 @@
         faces[side * face + size.fy : (side + 1) * face, :] = mids.astype(BF16)
 
 
-def prepare_kernel(size, both, after, *refs):
-    held = (len(refs) - 4) // 2
+def prepare_kernel(size, both, after, biases, head_scale, *refs):
+    held = (len(refs) - 5) // 2
     sources, targets = refs[:held], refs[held : 2 * held]
-    queries, fine, mid, sems = refs[2 * held :]
-    copies = fetch(sources, targets, sems)
+    queries, fine, mid, scale_here, sems = refs[2 * held :]
+    rows = mid.at[:, pl.ds(size.mid_rows, size.scale_at - size.mid_rows), :]
+    copies = fetch((*sources, head_scale, biases), (*targets, scale_here, rows), sems)
     cells = both[: size.cells, :].astype(F32)
     mids = both[size.cells :, :].astype(F32)
-    mid[...] = jnp.zeros_like(mid)
+    mid[:, : size.mid_rows, :] = jnp.zeros((size.parts, size.mid_rows, LANES), F32)
     for x in range(size.x):
         at = ((x + 1) * (size.y + 2) + 1) * size.z
         split_store(fine, slice(at, at + size.y * size.z), cells[x * size.y * size.z : (x + 1) * size.y * size.z])
@@ -190,6 +196,7 @@
     queries[...] = dot(both[: size.cells, :], targets[0][...]).astype(BF16)
     for copy in copies[1:]:
         copy.wait()
+    split_store(mid, slice(size.scale_at, size.scale_at + 1), lane_scale(size, scale_here))
 
 
 def pick(odd, from_a, from_b):
@@ -281,132 +288,140 @@
     return (weights * (1.0 / jnp.sum(weights, axis=0, keepdims=True))).astype(BF16)
 
 
+def tiled(scores, one):
+    length = one.shape[0]
+    return (scores.reshape(-1, length, scores.shape[-1]) + one[None]).reshape(scores.shape)
+
+
 def gather_heads(size, total, wide):
     return jnp.sum(total.reshape(HEADS, size.group, size.c) * wide, axis=0)
 
 
-def coarse_kernel(
-    size, head_scale, queries, fine, coarse, key_weight, value_weight, mask, coarse_out, keys, values, scale_here, sems
+def own_kernel(
+    size, kept, queries, fine, coarse, key_weight, value_weight, mask, coarse_out, fine_out, stats
 ):
-    copy = fetch((head_scale,), (scale_here,), sems)[0]
     block = joined(fine, slice(None)).astype(BF16)
-    keys[...] = dot(block, key_weight[...]).astype(BF16)
-    values[...] = dot(block, value_weight[...]).astype(BF16)
+    keys = dot(block, key_weight[...]).astype(BF16)
+    values = dot(block, value_weight[...]).astype(BF16)
     cells = coarse[...]
     coarse_keys = dot(cells, key_weight[...]).astype(BF16)
     coarse_values = dot(cells, value_weight[...]).astype(BF16)
-    copy.wait()
-    scale = lane_scale(size, scale_here)
+    scale = joined(kept, slice(size.scale_at, size.scale_at + 1))
     spread_mask = mask[...]
     wide = spread_mask.astype(F32).reshape(HEADS, size.group, size.c)
-    for bx, by in size.groups:
-        rows = size.query_rows(bx, by)
-        spread = spread_queries(size, queries, rows, spread_mask)
+    run_bias = joined(kept, slice(size.mid_rows, size.mid_rows + size.z))
+    fine_row = (size.y + 2) * size.z
+    for index, (bx, by) in enumerate(size.groups):
+        at = slice(index * size.group, (index + 1) * size.group)
+        spread = spread_queries(size, queries, size.query_rows(bx, by), spread_mask)
         total = dot_tn(soft(dot_nt(coarse_keys, spread) * scale), coarse_values)
-        result = gather_heads(size, total, wide)
-        for k, r in enumerate(rows):
-            coarse_out[r, :] = result[k * 2 * size.z : (k + 1) * 2 * size.z]
+        coarse_out[at, :] = gather_heads(size, total, wide)
+        slabs = [
+            slice((2 * bx + k) * fine_row + 2 * by * size.z, (2 * bx + k) * fine_row + (2 * by + 4) * size.z)
+            for k in range(4)
+        ]
+        some_keys = jnp.concatenate([keys[s] for s in slabs], axis=0)
+        some_values = jnp.concatenate([values[s] for s in slabs], axis=0)
+        scores = tiled(dot_nt(some_keys, spread) * scale, run_bias)
+        highest = jnp.max(scores, axis=0, keepdims=True)
+        weights = jnp.exp2(scores - highest)
+        stats[index : index + 1, :] = highest
+        stats[len(size.groups) + index : len(size.groups) + index + 1, :] = jnp.sum(weights, axis=0, keepdims=True)
+        fine_out[at, :] = gather_heads(size, dot_tn(weights.astype(BF16), some_values), wide)
 
 
 def last_kernel(
     size,
-    head_scale,
     tokens,
     mlp_gain,
-    biases,
+    out_weight,
+    up_weight,
+    down_weight,
     queries,
-    keys,
-    values,
     mid_in,
     from_a,
     from_b,
     coarse_out,
+    fine_out,
+    stats,
     key_weight,
     value_weight,
-    out_weight,
-    up_weight,
-    down_weight,
     mask,
     arrange,
     out,
     mid,
     attended,
-    scale_here,
+    joint,
+    factors,
     tokens_here,
     gain_here,
-    bias,
+    out_here,
+    up_here,
+    down_here,
     sems,
 ):
-    copies = fetch((biases, head_scale, tokens, mlp_gain), (bias, scale_here, tokens_here, gain_here), sems)
+    copies = fetch(
+        (tokens, mlp_gain, out_weight, up_weight, down_weight),
+        (tokens_here, gain_here, out_here, up_here, down_here),
+        sems,
+    )
     low, high = pick(is_odd("gz"), from_a, from_b)
-    mid[...] = mid_in[...]
+    mid[...] = mid_in[:, : size.mid_rows, :]
     split_store(mid, pl.ds(size.mz, size.gz, stride=size.mzp), low[size.fzp : size.fzp + size.gz])
     split_store(mid, pl.ds(size.mz + 1, size.gz, stride=size.mzp), high[size.fzp : size.fzp + size.gz])
     ends = jnp.concatenate([low[: size.fzp], high[: size.fzp]], axis=0).astype(BF16)
     ends = dot(arrange[...], ends).astype(BF16)
-    end_keys = dot(ends, key_weight[...]).astype(BF16)
-    end_values = dot(ends, value_weight[...]).astype(BF16)
     mids = joined(mid, slice(None)).astype(BF16)
-    mid_keys = dot(mids, key_weight[...]).astype(BF16)
-    mid_values = dot(mids, value_weight[...]).astype(BF16)
-
+    cells = jnp.concatenate([ends, mids], axis=0)
+    keys = dot(cells, key_weight[...]).astype(BF16)
+    values = dot(cells, value_weight[...]).astype(BF16)
+    scale = joined(mid_in, slice(size.scale_at, size.scale_at + 1))
+    spread_mask = mask[...]
+    wide = spread_mask.astype(F32).reshape(HEADS, size.group, size.c)
+    bias = joined(mid_in, slice(size.mid_rows + size.z, size.ones_at))
+    mid_bias, low_bias, high_bias = bias[: size.mzp], bias[size.mzp : size.mzp + 1], bias[size.mzp + 1 : size.mzp + 2]
+    ones = joined(mid_in, slice(size.ones_at, size.scale_at))
+    mid_row = (size.my + 2) * size.mzp
+    count = len(size.groups)
+
+    for index, (bx, by) in enumerate(size.groups):
+        at = slice(index * size.group, (index + 1) * size.group)
+        spread = spread_queries(size, queries, size.query_rows(bx, by), spread_mask)
+        ends_at = slice(32 * index, 32 * index + 32)
+        start = [
+            count * 32 + (2 * (bx // 2) + k) * mid_row + 2 * (by // 2) * size.mzp for k in range(4)
+        ]
+        slabs = [ends_at] + [slice(s, s + 4 * size.mzp) for s in start]
+        both = dot_nt(jnp.concatenate([keys[s] for s in slabs], axis=0), spread) * scale
+        scores = jnp.concatenate([both[:16] + low_bias, both[16:32] + high_bias], axis=0)
+        before = stats[index : index + 1, :]
+        highest = jnp.maximum(before, jnp.max(scores, axis=0, keepdims=True))
+        weights = jnp.exp2(scores - highest)
+        shrink = jnp.exp2(before - highest)
+        summed = stats[count + index : count + index + 1, :] * shrink + jnp.sum(weights, axis=0, keepdims=True)
+        inverse = 1.0 / summed
+        factor = ones * (shrink * inverse)
+        coarser = factor.astype(BF16)
+        factors[at, :] = coarser
+        finer = slice(count * size.group + at.start, count * size.group + at.stop)
+        factors[finer, :] = (factor - coarser.astype(F32)).astype(BF16)
+        weights = jnp.concatenate([(weights * inverse).astype(BF16), soft(tiled(both[32:], mid_bias))], axis=0)
+        total = dot_tn(weights, jnp.concatenate([values[s] for s in slabs], axis=0))
+        joint[at, :] = gather_heads(size, total, wide) + coarse_out[at, :]
+
+    spread_factors = dot(factors[...], spread_mask)
+    half = count * size.group
+    result = joint[...] + fine_out[...] * (spread_factors[:half] + spread_factors[half:])
+    for index, (bx, by) in enumerate(size.groups):
+        part = result[index * size.group : (index + 1) * size.group].astype(BF16)
+        for k, r in enumerate(size.query_rows(bx, by)):
+            attended[r, :] = part[k * 2 * size.z : (k + 1) * 2 * size.z]
     for copy in copies:
         copy.wait()
-    scale = lane_scale(size, scale_here)
-    spread_mask = mask[...]
-    wide = spread_mask.astype(F32).reshape(HEADS, size.group, size.c)
-    run_bias = bias[: size.z]
-    mid_bias = bias[size.z : size.z + size.mzp]
-    low_bias = bias[size.z + size.mzp : size.z + size.mzp + 1]
-    high_bias = bias[size.z + size.mzp + 1 : size.z + size.mzp + 2]
-    fine_row = (size.y + 2) * size.z
-    mid_row = (size.my + 2) * size.mzp
-
-    def tiled(scores, one):
-        length = one.shape[0]
-        return (scores.reshape(-1, length, scores.shape[-1]) + one[None]).reshape(scores.shape)
-
-    for index, (bx, by) in enumerate(size.groups):
-        rows = size.query_rows(bx, by)
-        spread = spread_queries(size, queries, rows, spread_mask)
-        slabs = [
-            slice((2 * bx + k) * fine_row + 2 * by * size.z, (2 * bx + k) * fine_row + (2 * by + 4) * size.z)
-            for k in range(4)
-        ]
-        ends_at = slice(32 * index, 32 * index + 32)
-        some_keys = jnp.concatenate([keys[s, :] for s in slabs] + [end_keys[ends_at]], axis=0)
-        some_values = jnp.concatenate([values[s, :] for s in slabs] + [end_values[ends_at]], axis=0)
-        scores = dot_nt(some_keys, spread) * scale
-        inner = 16 * size.z
-        scores = jnp.concatenate(
-            [
-                tiled(scores[:inner], run_bias),
-                scores[inner : inner + 16] + low_bias,
-                scores[inner + 16 :] + high_bias,
-            ],
-            axis=0,
-        )
-        total = dot_tn(soft(scores), some_values)
-        slabs = [
-            slice(
-                (2 * (bx // 2) + k) * mid_row + 2 * (by // 2) * size.mzp,
-                (2 * (bx // 2) + k) * mid_row + (2 * (by // 2) + 4) * size.mzp,
-            )
-            for k in range(4)
-        ]
-        some_keys = jnp.concatenate([mid_keys[s] for s in slabs], axis=0)
-        some_values = jnp.concatenate([mid_values[s] for s in slabs], axis=0)
-        scores = tiled(dot_nt(some_keys, spread) * scale, mid_bias)
-        total = total + dot_tn(soft(scores), some_values)
-        result = gather_heads(size, total, wide)
-        for k, r in enumerate(rows):
-            part = result[k * 2 * size.z : (k + 1) * 2 * size.z]
-            attended[r, :] = (part + coarse_out[r, :]).astype(BF16)
-
-    residual = (tokens_here[...].astype(F32) + dot(attended[...], out_weight[...])).astype(BF16)
+    residual = (tokens_here[...].astype(F32) + dot(attended[...], out_here[...])).astype(BF16)
     second = layer_norm(residual.astype(F32), gain_here[...])
-    hidden = jax.nn.gelu(dot(second, up_weight[...]), approximate=True).astype(BF16)
-    out[...] = (residual.astype(F32) + dot(hidden, down_weight[...])).astype(BF16)
+    hidden = jax.nn.gelu(dot(second, up_here[...]), approximate=True).astype(BF16)
+    out[...] = (residual.astype(F32) + dot(hidden, down_here[...])).astype(BF16)
 
 
 def swap(array, axis, start):
@@ -487,32 +502,32 @@
         value_weight,
         head_mask(size),
         arranging(size),
-        out_weight,
-        up_weight,
-        down_weight,
-    )
+    )
+    late = pinned(out_weight, up_weight, down_weight)
     *weights, queries, fine, mid = call(
         functools.partial(prepare_kernel, size),
         [(a.shape, a.dtype) for a in held]
         + [
             ((size.cells, channels), BF16),
             ((size.parts, size.fine_rows, LANES), F32),
-            ((size.parts, size.mid_rows, LANES), F32),
+            ((size.parts, size.kept_rows, LANES), F32),
         ],
         both,
         face_a,
+        biases,
+        scales,
         *held,
-        spaces=[vmem] * 2 + [hbm] * len(held),
-        scratch=[pltpu.SemaphoreType.DMA((len(held),))],
-    )
-    wq, wk, wv, mask, arrange, wo, wu, wd = weights
+        spaces=[vmem] * 2 + [hbm] * (2 + len(held)),
+        scratch=[pltpu.SMEM((HEADS,), F32), pltpu.SemaphoreType.DMA((2 + len(held),))],
+    )
+    wq, wk, wv, mask, arrange = weights
     z_a, z_b, fine, mid = call(
         functools.partial(z_kernel, size),
         [
             ((face_z, channels), BF16),
             ((face_z, channels), BF16),
             ((size.parts, size.fine_rows, LANES), F32),
-            ((size.parts, size.mid_rows, LANES), F32),
+            ((size.parts, size.kept_rows, LANES), F32),
         ],
         fine,
         mid,
@@ -523,53 +538,49 @@
     )
     got_a = swap(z_a, "gz", 0)
     got_b = swap(z_b, "gz", 1)
-    coarse_out, keys, values = call(
-        functools.partial(coarse_kernel, size),
+    lanes = HEADS * size.group
+    coarse_out, fine_out, stats = call(
+        functools.partial(own_kernel, size),
         [
             ((size.cells, channels), F32),
-            ((size.fine_rows, channels), BF16),
-            ((size.fine_rows, channels), BF16),
+            ((size.cells, channels), F32),
+            ((2 * len(size.groups), lanes), F32),
         ],
-        scales,
+        mid,
         queries,
         fine,
         gathered,
         wk,
         wv,
         mask,
-        spaces=[hbm] + [vmem] * 6,
-        scratch=[pltpu.SMEM((HEADS,), F32), pltpu.SemaphoreType.DMA((1,))],
     )
     out = call(
         functools.partial(last_kernel, size),
         [((size.cells, channels), BF16)],
-        scales,
         flat,
         gain_mlp,
-        biases,
+        *late,
         queries,
-        keys,
-        values,
         mid,
         got_a,
         got_b,
         coarse_out,
+        fine_out,
+        stats,
         wk,
         wv,
-        wo,
-        wu,
-        wd,
         mask,
         arrange,
-        spaces=[hbm] * 4 + [vmem] * 14,
+        spaces=[hbm] * 5 + [vmem] * 11,
         scratch=[
             pltpu.VMEM((size.parts, size.mid_rows, LANES), F32),
             pltpu.VMEM((size.cells, channels), BF16),
-            pltpu.SMEM((HEADS,), F32),
+            pltpu.VMEM((size.cells, channels), F32),
+            pltpu.VMEM((2 * size.cells, lanes), BF16),
             pltpu.VMEM(flat.shape, BF16),
             pltpu.VMEM(gain_mlp.shape, F32),
-            pltpu.VMEM(biases.shape, F32),
-            pltpu.SemaphoreType.DMA((4,)),
+            *[pltpu.VMEM(a.shape, BF16) for a in late],
+            pltpu.SemaphoreType.DMA((5,)),
         ],
         vmem=False,
     )[0]

time: 29.3 us -> 27.8 us (0.949)
  Pallas kernels: 12.6 us -> 11.6 us
  waiting for transfers between devices: 1.67 us -> 1.19 us
    pallas_call x6, Pallas kernels: 12.6 us -> 11.6 us  [call(): pl.pallas_call(kernel, out_shape=kinds, in_specs=[pl.BlockSpec(memory_spa...]
    ppermute x5, waiting for transfers between devices: 1.66 us -> 1.19 us  [swap(): return lax.ppermute(array, axis, pairs)]
  transfers between devices with their start and end apart: 6 -> 6, of which waited for: 2 -> 2; matrix products, arithmetic and copies ran while one was open for 0% -> 0% of each run, Pallas kernels for 17% -> 19%
where the time goes in v2:
time: 27.8 us; the launch traced here: 27.6 us
  starting transfers between devices  14.7 us (53%)
  Pallas kernels  11.6 us (42%)
  waiting for transfers between devices  1.19 us (4%)
    pallas_call x6, Pallas kernels, call(): pl.pallas_call(kernel, out_shape=kinds, in_specs=[pl.BlockSpec(memory_spa...  11.6 us
    ppermute x5, starting transfers between devices, swap(): return lax.ppermute(array, axis, pairs)  9.82 us
    all_to_all x1, starting transfers between devices, shards(): lax.all_to_all(coarse.reshape(devices, size.coarse, channels), AXES, 0, 0)  4.92 us
    ppermute x5, waiting for transfers between devices, swap(): return lax.ppermute(array, axis, pairs)  1.19 us
  transfers between devices with their start and end apart: 6, of which 2 were waited for; matrix products, arithmetic and copies ran while one was open for 0% of the time, Pallas kernels for 19%

profile of v2, /device:TPU:0, one launch (start us, length us, event | category | flops | bytes accessed | tf_op | source)
XLA Modules:
  0.0 27.6 jit_solution(6525750602424009131)
XLA Ops:
  0.0 2.1 %shard_map.136 = (bf16[576,256]{1,0:T(8,128)(2,1)S(1)}, bf16[160,256]{1,0:T(8,128)(2,1)S(1)}, bf16[256,256]{1,0:T(8,128)(2,1)}) custom-call(bf16[512,256]{1,0:T(8,128)(2,1)} %bitcast.7, f32[1,256]{1,0:T(1,128)} %bitcast.9, bf16[112,512]{1,0:T(8,128)(2,1)} %constant.9.clone.pool), custom_call_target="tpu_custom_call" | custom-call | tf_op jit(solution)/shard_map/pallas_call | solution.py:57
  2.1 3.0 %collective-permute-start = (bf16[160,256]{1,0:T(8,128)(2,1)S(1)}, bf16[160,256]{1,0:T(8,128)(2,1)S(1)}, u32[]{:S(2)}, u32[]{:S(2)}) collective-permute-start(bf16[160,256]{1,0:T(8,128)(2,1)S(1)} %get-tuple-element.25), channel_id=1, source_target_pairs={{0,4},{4,0},{1,5},{5,1},{2,6},{6,2},{3,7},{7,3},{8,12},{12,8},{9,1... | collective-permute-start | bytes 245768 | tf_op jit(solution)/shard_map/ppermute | solution.py:433
  5.1 4.9 %all-to-all-start = ((bf16[32,8,256]{2,1,0:T(8,128)(2,1)}), bf16[32,8,256]{2,1,0:T(8,128)(2,1)S(1)}, u32[]{:S(2)}, u32[]{:S(2)}) async-start(bf16[32,8,256]{2,1,0:T(8,128)(2,1)} %bitcast.3), calls=%async_computation | async-start | bytes 262144 | tf_op jit(solution)/shard_map/all_to_all | solution.py:489
  10.0 0.0 collective-permute-done.refs_0_
  10.1 1.6 %collective-permute-start.2 = (bf16[104,256]{1,0:T(8,128)(2,1)S(1)}, bf16[104,256]{1,0:T(8,128)(2,1)S(1)}, u32[]{:S(2)}, u32[]{:S(2)}) collective-permute-start(bf16[104,256]{1,0:T(8,128)(2,1)S(1)} %get-tuple-element.30), channel_id=1, source_target_pairs={{8,16},{16,8},{24,0},{0,24},{9,17},{17,9},{25,1},{1,25},{10,18},{1... | collective-permute-start | bytes 159752 | tf_op jit(solution)/shard_map/ppermute | solution.py:433
  11.6 0.4 %collective-permute-start.1 = (bf16[104,256]{1,0:T(8,128)(2,1)S(1)}, bf16[104,256]{1,0:T(8,128)(2,1)S(1)}, u32[]{:S(2)}, u32[]{:S(2)}) collective-permute-start(bf16[104,256]{1,0:T(8,128)(2,1)S(1)} %get-tuple-element.26.after), channel_id=1, source_target_pairs={{0,8},{8,0},{16,24},{24,16},{1,9},{9,1},{17,25},{25,17},{2,10},{10... | collective-permute-start | bytes 159752 | tf_op jit(solution)/shard_map/ppermute | solution.py:433
  12.0 1.9 %shard_map.138 = (bf16[256,256]{1,0:T(8,128)(2,1)}, bf16[256,256]{1,0:T(8,128)(2,1)S(1)}, bf16[256,256]{1,0:T(8,128)(2,1)S(1)}, bf16[256,256]{1,0:T(8,128)(2,1)S...) custom-call(bf16[576,256]{1,0:T(8,128)(2,1)S(1)} %get-tuple-element., ...), custom_call_target="tpu_custom_call" | custom-call | tf_op jit(solution)/shard_map/pallas_call | solution.py:57
  13.9 0.3 collective-permute-done.2.from_b
  14.2 0.0 collective-permute-done.1.from_a
  14.2 0.1 shard_map.139
  14.3 2.1 %collective-permute-start.3 = (bf16[144,256]{1,0:T(8,128)(2,1)S(1)}, bf16[144,256]{1,0:T(8,128)(2,1)S(1)}, u32[]{:S(2)}, u32[]{:S(2)}) collective-permute-start(bf16[144,256]{1,0:T(8,128)(2,1)S(1)} %get-tuple-element.32), channel_id=1, source_target_pairs={{0,1},{1,0},{2,3},{3,2},{4,5},{5,4},{6,7},{7,6},{8,9},{9,8},{10,11... | collective-permute-start | bytes 221192 | tf_op jit(solution)/shard_map/ppermute | solution.py:433
  16.4 2.8 %collective-permute-start.4 = (bf16[144,256]{1,0:T(8,128)(2,1)S(1)}, bf16[144,256]{1,0:T(8,128)(2,1)S(1)}, u32[]{:S(2)}, u32[]{:S(2)}) collective-permute-start(bf16[144,256]{1,0:T(8,128)(2,1)S(1)} %get-tuple-element.33), channel_id=1, source_target_pairs={{1,2},{2,1},{3,0},{0,3},{5,6},{6,5},{7,4},{4,7},{9,10},{10,9},{11,... | collective-permute-start | bytes 221192 | tf_op jit(solution)/shard_map/ppermute | solution.py:433
  19.2 0.0 all-to-all-done
  19.2 3.3 %shard_map.140 = (f32[512,256]{1,0:T(8,128)S(1)}, f32[512,256]{1,0:T(8,128)S(1)}, f32[32,256]{1,0:T(8,128)S(1)}) custom-call(f32[2,352,128]{2,1,0:T(8,128)S(1)} %get-tuple-element.31.kept.mid_in, bf16[512,256]{1,0:T(8,128)(2,1)S(1)} %get-tuple-element.27.queries, f32[2,800,128]{2,1,0:T(8,128)S(1)} %get-tuple-element.34.fine, bf16[256,256]{1,0:T(8,128)(2,1)S(1)} %bitcast.6, ...), custom_call_target="tpu_custom_call" | custom-call | tf_op jit(solution)/shard_map/pallas_call | solution.py:57
  22.5 0.0 collective-permute-done.3.from_a
  22.5 0.9 %collective-permute-done.4.from_b = bf16[144,256]{1,0:T(8,128)(2,1)S(1)} collective-permute-done((bf16[144,256]{1,0:T(8,128)(2,1)S(1)}, bf16[144,256]{1,0:T(8,128)(2,1)S(1)}, u32[]{:S(2)}, u32[]{:S(2)}) %collective-permute-start.4) | collective-permute-done | bytes 73760 | tf_op jit(solution)/shard_map/ppermute | solution.py:433
  23.4 4.2 %shard_map.141 = bf16[512,256]{1,0:T(8,128)(2,1)} custom-call(bf16[512,256]{1,0:T(8,128)(2,1)} %bitcast.8, f32[1,256]{1,0:T(1,128)} %bitcast.10, bf16[256,256]{1,0:T(8,128)(2,1)} %out_weight.1, bf16[256,512]{1,0:T(8,128)(2,1)} %up_weight.1, bf16[512,256]{1,0:T(8,128)(2,1)} %down_weight.1, bf16[512,256]{1,0:T(8,128)(2,1)S(1)} %get-tuple-element.27.queries, ...), custom_call_target="tpu_custom_call" | custom-call | tf_op jit(solution)/shard_map/pallas_call | solution.py:57
  (1 shorter events, 0.0 us)
Async XLA Ops:
  2.1 7.9 %collective-permute-start = (bf16[160,256]{1,0:T(8,128)(2,1)S(1)}, bf16[160,256]{1,0:T(8,128)(2,1)S(1)}, u32[]{:S(2)}, u32[]{:S(2)}) collective-permute-start(bf16[160,256]{1,0:T(8,128)(2,1)S(1)} %get-tuple-element.25), channel_id=1, source_target_pairs={{0,4},{4,0},{1,5},{5,1},{2,6},{6,2},{3,7},{7,3},{8,12},{12,8},{9,1... | collective-permute-start | bytes 245768 | tf_op jit(solution)/shard_map/ppermute | solution.py:433
  5.1 14.1 %all-to-all-start = ((bf16[32,8,256]{2,1,0:T(8,128)(2,1)}), bf16[32,8,256]{2,1,0:T(8,128)(2,1)S(1)}, u32[]{:S(2)}, u32[]{:S(2)}) async-start(bf16[32,8,256]{2,1,0:T(8,128)(2,1)} %bitcast.3), calls=%async_computation | async-start | bytes 262144 | tf_op jit(solution)/shard_map/all_to_all | solution.py:489
  10.1 4.1 %collective-permute-start.2 = (bf16[104,256]{1,0:T(8,128)(2,1)S(1)}, bf16[104,256]{1,0:T(8,128)(2,1)S(1)}, u32[]{:S(2)}, u32[]{:S(2)}) collective-permute-start(bf16[104,256]{1,0:T(8,128)(2,1)S(1)} %get-tuple-element.30), channel_id=1, source_target_pairs={{8,16},{16,8},{24,0},{0,24},{9,17},{17,9},{25,1},{1,25},{10,18},{1... | collective-permute-start | bytes 159752 | tf_op jit(solution)/shard_map/ppermute | solution.py:433
  11.6 2.6 %collective-permute-start.1 = (bf16[104,256]{1,0:T(8,128)(2,1)S(1)}, bf16[104,256]{1,0:T(8,128)(2,1)S(1)}, u32[]{:S(2)}, u32[]{:S(2)}) collective-permute-start(bf16[104,256]{1,0:T(8,128)(2,1)S(1)} %get-tuple-element.26.after), channel_id=1, source_target_pairs={{0,8},{8,0},{16,24},{24,16},{1,9},{9,1},{17,25},{25,17},{2,10},{10... | collective-permute-start | bytes 159752 | tf_op jit(solution)/shard_map/ppermute | solution.py:433
  14.3 8.2 %collective-permute-start.3 = (bf16[144,256]{1,0:T(8,128)(2,1)S(1)}, bf16[144,256]{1,0:T(8,128)(2,1)S(1)}, u32[]{:S(2)}, u32[]{:S(2)}) collective-permute-start(bf16[144,256]{1,0:T(8,128)(2,1)S(1)} %get-tuple-element.32), channel_id=1, source_target_pairs={{0,1},{1,0},{2,3},{3,2},{4,5},{5,4},{6,7},{7,6},{8,9},{9,8},{10,11... | collective-permute-start | bytes 221192 | tf_op jit(solution)/shard_map/ppermute | solution.py:433
  16.4 7.0 %collective-permute-start.4 = (bf16[144,256]{1,0:T(8,128)(2,1)S(1)}, bf16[144,256]{1,0:T(8,128)(2,1)S(1)}, u32[]{:S(2)}, u32[]{:S(2)}) collective-permute-start(bf16[144,256]{1,0:T(8,128)(2,1)S(1)} %get-tuple-element.33), channel_id=1, source_target_pairs={{1,2},{2,1},{3,0},{0,3},{5,6},{6,5},{7,4},{4,7},{9,10},{10,9},{11,... | collective-permute-start | bytes 221192 | tf_op jit(solution)/shard_map/ppermute | solution.py:433

commit v3 on v2

--- a/solution.py
+++ b/solution.py
@@ -85,7 +85,7 @@
         self.fy, self.gy = self.x * self.z, self.mx * self.mz
         self.fx, self.gx = (self.y + 2) * self.z, (self.my + 2) * self.mz
         self.fz, self.gz = (self.x + 2) * (self.y + 2), (self.mx + 2) * (self.my + 2)
-        self.fzp, self.gzp = up_to(self.fz, 8), up_to(self.gz, 8)
+        self.fzp, self.gzp = self.fz, self.gz
         self.groups = [(bx, by) for bx in range(self.x // 2) for by in range(self.y // 2)]
         self.group = 4 * self.z
 
@@ -293,8 +293,20 @@
     return (scores.reshape(-1, length, scores.shape[-1]) + one[None]).reshape(scores.shape)
 
 
-def gather_heads(size, total, wide):
-    return jnp.sum(total.reshape(HEADS, size.group, size.c) * wide, axis=0)
+def gather_heads(size, total):
+    heads, width = HEADS // size.parts, size.c // HEADS
+    lane = lax.broadcasted_iota(jnp.int32, (size.group, LANES), 1)
+    parts = []
+    for j in range(size.parts):
+        blocks = [
+            total[(j * heads + h) * size.group : (j * heads + h + 1) * size.group, j * LANES : (j + 1) * LANES]
+            for h in range(heads)
+        ]
+        result = blocks[0]
+        for h in range(1, heads):
+            result = jnp.where(lane >= h * width, blocks[h], result)
+        parts.append(result)
+    return jnp.concatenate(parts, axis=1)
 
 
 def own_kernel(
@@ -308,14 +320,13 @@
     coarse_values = dot(cells, value_weight[...]).astype(BF16)
     scale = joined(kept, slice(size.scale_at, size.scale_at + 1))
     spread_mask = mask[...]
-    wide = spread_mask.astype(F32).reshape(HEADS, size.group, size.c)
     run_bias = joined(kept, slice(size.mid_rows, size.mid_rows + size.z))
     fine_row = (size.y + 2) * size.z
     for index, (bx, by) in enumerate(size.groups):
         at = slice(index * size.group, (index + 1) * size.group)
         spread = spread_queries(size, queries, size.query_rows(bx, by), spread_mask)
         total = dot_tn(soft(dot_nt(coarse_keys, spread) * scale), coarse_values)
-        coarse_out[at, :] = gather_heads(size, total, wide)
+        coarse_out[at, :] = gather_heads(size, total)
         slabs = [
             slice((2 * bx + k) * fine_row + 2 * by * size.z, (2 * bx + k) * fine_row + (2 * by + 4) * size.z)
             for k in range(4)
@@ -327,7 +338,17 @@
         weights = jnp.exp2(scores - highest)
         stats[index : index + 1, :] = highest
         stats[len(size.groups) + index : len(size.groups) + index + 1, :] = jnp.sum(weights, axis=0, keepdims=True)
-        fine_out[at, :] = gather_heads(size, dot_tn(weights.astype(BF16), some_values), wide)
+        fine_out[at, :] = gather_heads(size, dot_tn(weights.astype(BF16), some_values))
+
+
+def weigh_heads(size, total, wide):
+    heads = HEADS // size.parts
+    parts = []
+    for j in range(size.parts):
+        rows = slice(j * heads * size.group, (j + 1) * heads * size.group)
+        cut = total[rows, j * LANES : (j + 1) * LANES].reshape(heads, size.group, LANES)
+        parts.append(jnp.sum(cut * wide[:heads, :, :LANES], axis=0))
+    return jnp.concatenate(parts, axis=1)
 
 
 def last_kernel(
@@ -407,7 +428,7 @@
         factors[finer, :] = (factor - coarser.astype(F32)).astype(BF16)
         weights = jnp.concatenate([(weights * inverse).astype(BF16), soft(tiled(both[32:], mid_bias))], axis=0)
         total = dot_tn(weights, jnp.concatenate([values[s] for s in slabs], axis=0))
-        joint[at, :] = gather_heads(size, total, wide) + coarse_out[at, :]
+        joint[at, :] = weigh_heads(size, total, wide) + coarse_out[at, :]
 
     spread_factors = dot(factors[...], spread_mask)
     half = count * size.group

time: 27.8 us -> 27.6 us (level)
  no operation moved by 1% of the time
where the time goes in v3:
time: 27.6 us; the launch traced here: 27.4 us
  starting transfers between devices  14.7 us (53%)
  Pallas kernels  11.5 us (42%)
  waiting for transfers between devices  1.09 us (4%)
    pallas_call x6, Pallas kernels, call(): pl.pallas_call(kernel, out_shape=kinds, in_specs=[pl.BlockSpec(memory_spa...  11.5 us
    ppermute x5, starting transfers between devices, swap(): return lax.ppermute(array, axis, pairs)  9.82 us
    all_to_all x1, starting transfers between devices, shards(): lax.all_to_all(coarse.reshape(devices, size.coarse, channels), AXES, 0, 0)  4.92 us
    ppermute x5, waiting for transfers between devices, swap(): return lax.ppermute(array, axis, pairs)  1.08 us
  transfers between devices with their start and end apart: 6, of which 2 were waited for; matrix products, arithmetic and copies ran while one was open for 0% of the time, Pallas kernels for 19%

profile of v3, /device:TPU:0, one launch (start us, length us, event | category | flops | bytes accessed | tf_op | source)
XLA Modules:
  0.0 27.4 jit_solution(1677793219674583774)
XLA Ops:
  0.0 2.1 %shard_map.136 = (bf16[576,256]{1,0:T(8,128)(2,1)S(1)}, bf16[160,256]{1,0:T(8,128)(2,1)S(1)}, bf16[256,256]{1,0:T(8,128)(2,1)}) custom-call(bf16[512,256]{1,0:T(8,128)(2,1)} %bitcast.7, f32[1,256]{1,0:T(1,128)} %bitcast.9, bf16[112,512]{1,0:T(8,128)(2,1)} %constant.9.clone.pool), custom_call_target="tpu_custom_call" | custom-call | tf_op jit(solution)/shard_map/pallas_call | solution.py:57
  2.1 3.0 %collective-permute-start = (bf16[160,256]{1,0:T(8,128)(2,1)S(1)}, bf16[160,256]{1,0:T(8,128)(2,1)S(1)}, u32[]{:S(2)}, u32[]{:S(2)}) collective-permute-start(bf16[160,256]{1,0:T(8,128)(2,1)S(1)} %get-tuple-element.25), channel_id=1, source_target_pairs={{0,4},{4,0},{1,5},{5,1},{2,6},{6,2},{3,7},{7,3},{8,12},{12,8},{9,1... | collective-permute-start | bytes 245768 | tf_op jit(solution)/shard_map/ppermute | solution.py:454
  5.1 4.9 %all-to-all-start = ((bf16[32,8,256]{2,1,0:T(8,128)(2,1)}), bf16[32,8,256]{2,1,0:T(8,128)(2,1)S(1)}, u32[]{:S(2)}, u32[]{:S(2)}) async-start(bf16[32,8,256]{2,1,0:T(8,128)(2,1)} %bitcast.3), calls=%async_computation | async-start | bytes 262144 | tf_op jit(solution)/shard_map/all_to_all | solution.py:510
  10.0 0.0 collective-permute-done.refs_0_
  10.1 1.6 %collective-permute-start.2 = (bf16[104,256]{1,0:T(8,128)(2,1)S(1)}, bf16[104,256]{1,0:T(8,128)(2,1)S(1)}, u32[]{:S(2)}, u32[]{:S(2)}) collective-permute-start(bf16[104,256]{1,0:T(8,128)(2,1)S(1)} %get-tuple-element.30), channel_id=1, source_target_pairs={{8,16},{16,8},{24,0},{0,24},{9,17},{17,9},{25,1},{1,25},{10,18},{1... | collective-permute-start | bytes 159752 | tf_op jit(solution)/shard_map/ppermute | solution.py:454
  11.6 0.4 %collective-permute-start.1 = (bf16[104,256]{1,0:T(8,128)(2,1)S(1)}, bf16[104,256]{1,0:T(8,128)(2,1)S(1)}, u32[]{:S(2)}, u32[]{:S(2)}) collective-permute-start(bf16[104,256]{1,0:T(8,128)(2,1)S(1)} %get-tuple-element.26.after), channel_id=1, source_target_pairs={{0,8},{8,0},{16,24},{24,16},{1,9},{9,1},{17,25},{25,17},{2,10},{10... | collective-permute-start | bytes 159752 | tf_op jit(solution)/shard_map/ppermute | solution.py:454
  12.0 1.9 %shard_map.138 = (bf16[256,256]{1,0:T(8,128)(2,1)}, bf16[256,256]{1,0:T(8,128)(2,1)S(1)}, bf16[256,256]{1,0:T(8,128)(2,1)S(1)}, bf16[256,256]{1,0:T(8,128)(2,1)S...) custom-call(bf16[576,256]{1,0:T(8,128)(2,1)S(1)} %get-tuple-element., ...), custom_call_target="tpu_custom_call" | custom-call | tf_op jit(solution)/shard_map/pallas_call | solution.py:57
  13.9 0.3 collective-permute-done.2.from_b
  14.2 0.0 collective-permute-done.1.from_a
  14.2 0.1 shard_map.139
  14.3 2.1 %collective-permute-start.3 = (bf16[136,256]{1,0:T(8,128)(2,1)S(1)}, bf16[136,256]{1,0:T(8,128)(2,1)S(1)}, u32[]{:S(2)}, u32[]{:S(2)}) collective-permute-start(bf16[136,256]{1,0:T(8,128)(2,1)S(1)} %get-tuple-element.32), channel_id=1, source_target_pairs={{0,1},{1,0},{2,3},{3,2},{4,5},{5,4},{6,7},{7,6},{8,9},{9,8},{10,11... | collective-permute-start | bytes 208904 | tf_op jit(solution)/shard_map/ppermute | solution.py:454
  16.4 2.8 %collective-permute-start.4 = (bf16[136,256]{1,0:T(8,128)(2,1)S(1)}, bf16[136,256]{1,0:T(8,128)(2,1)S(1)}, u32[]{:S(2)}, u32[]{:S(2)}) collective-permute-start(bf16[136,256]{1,0:T(8,128)(2,1)S(1)} %get-tuple-element.33), channel_id=1, source_target_pairs={{1,2},{2,1},{3,0},{0,3},{5,6},{6,5},{7,4},{4,7},{9,10},{10,9},{11,... | collective-permute-start | bytes 208904 | tf_op jit(solution)/shard_map/ppermute | solution.py:454
  19.2 0.0 all-to-all-done
  19.2 3.2 %shard_map.140 = (f32[512,256]{1,0:T(8,128)S(1)}, f32[512,256]{1,0:T(8,128)S(1)}, f32[32,256]{1,0:T(8,128)S(1)}) custom-call(f32[2,352,128]{2,1,0:T(8,128)S(1)} %get-tuple-element.31.kept.mid_in, bf16[512,256]{1,0:T(8,128)(2,1)S(1)} %get-tuple-element.27.queries, f32[2,800,128]{2,1,0:T(8,128)S(1)} %get-tuple-element.34.fine, bf16[256,256]{1,0:T(8,128)(2,1)S(1)} %bitcast.6, ...), custom_call_target="tpu_custom_call" | custom-call | tf_op jit(solution)/shard_map/pallas_call | solution.py:57
  22.4 0.0 collective-permute-done.3.from_a
  22.4 0.8 %collective-permute-done.4.from_b = bf16[136,256]{1,0:T(8,128)(2,1)S(1)} collective-permute-done((bf16[136,256]{1,0:T(8,128)(2,1)S(1)}, bf16[136,256]{1,0:T(8,128)(2,1)S(1)}, u32[]{:S(2)}, u32[]{:S(2)}) %collective-permute-start.4) | collective-permute-done | bytes 69664 | tf_op jit(solution)/shard_map/ppermute | solution.py:454
  23.2 4.2 %shard_map.141 = bf16[512,256]{1,0:T(8,128)(2,1)} custom-call(bf16[512,256]{1,0:T(8,128)(2,1)} %bitcast.8, f32[1,256]{1,0:T(1,128)} %bitcast.10, bf16[256,256]{1,0:T(8,128)(2,1)} %out_weight.1, bf16[256,512]{1,0:T(8,128)(2,1)} %up_weight.1, bf16[512,256]{1,0:T(8,128)(2,1)} %down_weight.1, bf16[512,256]{1,0:T(8,128)(2,1)S(1)} %get-tuple-element.27.queries, ...), custom_call_target="tpu_custom_call" | custom-call | tf_op jit(solution)/shard_map/pallas_call | solution.py:57
  (1 shorter events, 0.0 us)
Async XLA Ops:
  2.1 7.9 %collective-permute-start = (bf16[160,256]{1,0:T(8,128)(2,1)S(1)}, bf16[160,256]{1,0:T(8,128)(2,1)S(1)}, u32[]{:S(2)}, u32[]{:S(2)}) collective-permute-start(bf16[160,256]{1,0:T(8,128)(2,1)S(1)} %get-tuple-element.25), channel_id=1, source_target_pairs={{0,4},{4,0},{1,5},{5,1},{2,6},{6,2},{3,7},{7,3},{8,12},{12,8},{9,1... | collective-permute-start | bytes 245768 | tf_op jit(solution)/shard_map/ppermute | solution.py:454
  5.1 14.1 %all-to-all-start = ((bf16[32,8,256]{2,1,0:T(8,128)(2,1)}), bf16[32,8,256]{2,1,0:T(8,128)(2,1)S(1)}, u32[]{:S(2)}, u32[]{:S(2)}) async-start(bf16[32,8,256]{2,1,0:T(8,128)(2,1)} %bitcast.3), calls=%async_computation | async-start | bytes 262144 | tf_op jit(solution)/shard_map/all_to_all | solution.py:510
  10.1 4.1 %collective-permute-start.2 = (bf16[104,256]{1,0:T(8,128)(2,1)S(1)}, bf16[104,256]{1,0:T(8,128)(2,1)S(1)}, u32[]{:S(2)}, u32[]{:S(2)}) collective-permute-start(bf16[104,256]{1,0:T(8,128)(2,1)S(1)} %get-tuple-element.30), channel_id=1, source_target_pairs={{8,16},{16,8},{24,0},{0,24},{9,17},{17,9},{25,1},{1,25},{10,18},{1... | collective-permute-start | bytes 159752 | tf_op jit(solution)/shard_map/ppermute | solution.py:454
  11.6 2.6 %collective-permute-start.1 = (bf16[104,256]{1,0:T(8,128)(2,1)S(1)}, bf16[104,256]{1,0:T(8,128)(2,1)S(1)}, u32[]{:S(2)}, u32[]{:S(2)}) collective-permute-start(bf16[104,256]{1,0:T(8,128)(2,1)S(1)} %get-tuple-element.26.after), channel_id=1, source_target_pairs={{0,8},{8,0},{16,24},{24,16},{1,9},{9,1},{17,25},{25,17},{2,10},{10... | collective-permute-start | bytes 159752 | tf_op jit(solution)/shard_map/ppermute | solution.py:454
  14.3 8.1 %collective-permute-start.3 = (bf16[136,256]{1,0:T(8,128)(2,1)S(1)}, bf16[136,256]{1,0:T(8,128)(2,1)S(1)}, u32[]{:S(2)}, u32[]{:S(2)}) collective-permute-start(bf16[136,256]{1,0:T(8,128)(2,1)S(1)} %get-tuple-element.32), channel_id=1, source_target_pairs={{0,1},{1,0},{2,3},{3,2},{4,5},{5,4},{6,7},{7,6},{8,9},{9,8},{10,11... | collective-permute-start | bytes 208904 | tf_op jit(solution)/shard_map/ppermute | solution.py:454
  16.4 6.8 %collective-permute-start.4 = (bf16[136,256]{1,0:T(8,128)(2,1)S(1)}, bf16[136,256]{1,0:T(8,128)(2,1)S(1)}, u32[]{:S(2)}, u32[]{:S(2)}) collective-permute-start(bf16[136,256]{1,0:T(8,128)(2,1)S(1)} %get-tuple-element.33), channel_id=1, source_target_pairs={{1,2},{2,1},{3,0},{0,3},{5,6},{6,5},{7,4},{4,7},{9,10},{10,9},{11,... | collective-permute-start | bytes 208904 | tf_op jit(solution)/shard_map/ppermute | solution.py:454

commit v4 on v3

--- a/solution.py
+++ b/solution.py
@@ -310,8 +310,11 @@
 
 
 def own_kernel(
-    size, kept, queries, fine, coarse, key_weight, value_weight, mask, coarse_out, fine_out, stats
+    size, kept, queries, fine, coarse, key_weight, value_weight, mask, *refs
 ):
+    late = (len(refs) - 4) // 2
+    sources, (coarse_out, fine_out, stats, *targets), sems = refs[:late], refs[late:-1], refs[-1]
+    copies = fetch(sources, targets, sems)
     block = joined(fine, slice(None)).astype(BF16)
     keys = dot(block, key_weight[...]).astype(BF16)
     values = dot(block, value_weight[...]).astype(BF16)
@@ -339,6 +342,8 @@
         stats[index : index + 1, :] = highest
         stats[len(size.groups) + index : len(size.groups) + index + 1, :] = jnp.sum(weights, axis=0, keepdims=True)
         fine_out[at, :] = gather_heads(size, dot_tn(weights.astype(BF16), some_values))
+    for copy in copies:
+        copy.wait()
 
 
 def weigh_heads(size, total, wide):
@@ -353,11 +358,7 @@
 
 def last_kernel(
     size,
-    tokens,
     mlp_gain,
-    out_weight,
-    up_weight,
-    down_weight,
     queries,
     mid_in,
     from_a,
@@ -369,23 +370,19 @@
     value_weight,
     mask,
     arrange,
+    tokens_here,
+    out_here,
+    up_here,
+    down_here,
     out,
     mid,
     attended,
     joint,
     factors,
-    tokens_here,
     gain_here,
-    out_here,
-    up_here,
-    down_here,
     sems,
 ):
-    copies = fetch(
-        (tokens, mlp_gain, out_weight, up_weight, down_weight),
-        (tokens_here, gain_here, out_here, up_here, down_here),
-        sems,
-    )
+    copies = fetch((mlp_gain,), (gain_here,), sems)
     low, high = pick(is_odd("gz"), from_a, from_b)
     mid[...] = mid_in[:, : size.mid_rows, :]
     split_store(mid, pl.ds(size.mz, size.gz, stride=size.mzp), low[size.fzp : size.fzp + size.gz])
@@ -560,13 +557,15 @@
     got_a = swap(z_a, "gz", 0)
     got_b = swap(z_b, "gz", 1)
     lanes = HEADS * size.group
-    coarse_out, fine_out, stats = call(
+    late = [flat, *late]
+    coarse_out, fine_out, stats, *late_here = call(
         functools.partial(own_kernel, size),
         [
             ((size.cells, channels), F32),
             ((size.cells, channels), F32),
             ((2 * len(size.groups), lanes), F32),
-        ],
+        ]
+        + [(a.shape, a.dtype) for a in late],
         mid,
         queries,
         fine,
@@ -574,13 +573,14 @@
         wk,
         wv,
         mask,
+        *late,
+        spaces=[vmem] * 7 + [hbm] * len(late),
+        scratch=[pltpu.SemaphoreType.DMA((len(late),))],
     )
     out = call(
         functools.partial(last_kernel, size),
         [((size.cells, channels), BF16)],
-        flat,
         gain_mlp,
-        *late,
         queries,
         mid,
         got_a,
@@ -592,16 +592,15 @@
         wv,
         mask,
         arrange,
-        spaces=[hbm] * 5 + [vmem] * 11,
+        *late_here,
+        spaces=[hbm] + [vmem] * 15,
         scratch=[
             pltpu.VMEM((size.parts, size.mid_rows, LANES), F32),
             pltpu.VMEM((size.cells, channels), BF16),
             pltpu.VMEM((size.cells, channels), F32),
             pltpu.VMEM((2 * size.cells, lanes), BF16),
-            pltpu.VMEM(flat.shape, BF16),
             pltpu.VMEM(gain_mlp.shape, F32),
-            *[pltpu.VMEM(a.shape, BF16) for a in late],
-            pltpu.SemaphoreType.DMA((5,)),
+            pltpu.SemaphoreType.DMA((1,)),
         ],
         vmem=False,
     )[0]

time: 27.6 us -> 27.8 us (level)
  Pallas kernels: 11.5 us -> 12.4 us
  waiting for transfers between devices: 1.09 us -> 0.28 us
    pallas_call x6, Pallas kernels: 11.5 us -> 12.4 us  [call(): pl.pallas_call(kernel, out_shape=kinds, in_specs=[pl.BlockSpec(memory_spa...]
    ppermute x5, waiting for transfers between devices: 1.08 us -> 0.28 us  [swap(): return lax.ppermute(array, axis, pairs)]
  transfers between devices with their start and end apart: 6 -> 6, of which waited for: 2 -> 1; matrix products, arithmetic and copies ran while one was open for 0% -> 0% of each run, Pallas kernels for 19% -> 23%
where the time goes in v4:
time: 27.8 us; the launch traced here: 27.5 us
  starting transfers between devices  14.7 us (53%)
  Pallas kernels  12.4 us (45%)
  waiting for transfers between devices  0.28 us (1%)
    pallas_call x6, Pallas kernels, call(): pl.pallas_call(kernel, out_shape=kinds, in_specs=[pl.BlockSpec(memory_spa...  12.4 us
    ppermute x5, starting transfers between devices, swap(): return lax.ppermute(array, axis, pairs)  9.82 us
    all_to_all x1, starting transfers between devices, shards(): lax.all_to_all(coarse.reshape(devices, size.coarse, channels), AXES, 0, 0)  4.92 us
  transfers between devices with their start and end apart: 6, of which 1 were waited for; matrix products, arithmetic and copies ran while one was open for 0% of the time, Pallas kernels for 23%

profile of v4, /device:TPU:0, one launch (start us, length us, event | category | flops | bytes accessed | tf_op | source)
XLA Modules:
  0.0 27.5 jit_solution(15879383778307809929)
XLA Ops:
  0.0 2.1 %shard_map.136 = (bf16[576,256]{1,0:T(8,128)(2,1)S(1)}, bf16[160,256]{1,0:T(8,128)(2,1)S(1)}, bf16[256,256]{1,0:T(8,128)(2,1)}) custom-call(bf16[512,256]{1,0:T(8,128)(2,1)} %bitcast.7, f32[1,256]{1,0:T(1,128)} %bitcast.9, bf16[112,512]{1,0:T(8,128)(2,1)} %constant.9.clone.pool), custom_call_target="tpu_custom_call" | custom-call | tf_op jit(solution)/shard_map/pallas_call | solution.py:57
  2.1 3.0 %collective-permute-start = (bf16[160,256]{1,0:T(8,128)(2,1)S(1)}, bf16[160,256]{1,0:T(8,128)(2,1)S(1)}, u32[]{:S(2)}, u32[]{:S(2)}) collective-permute-start(bf16[160,256]{1,0:T(8,128)(2,1)S(1)} %get-tuple-element.29), channel_id=1, source_target_pairs={{0,4},{4,0},{1,5},{5,1},{2,6},{6,2},{3,7},{7,3},{8,12},{12,8},{9,1... | collective-permute-start | bytes 245768 | tf_op jit(solution)/shard_map/ppermute | solution.py:451
  5.1 4.9 %all-to-all-start = ((bf16[32,8,256]{2,1,0:T(8,128)(2,1)}), bf16[32,8,256]{2,1,0:T(8,128)(2,1)S(1)}, u32[]{:S(2)}, u32[]{:S(2)}) async-start(bf16[32,8,256]{2,1,0:T(8,128)(2,1)} %bitcast.3), calls=%async_computation | async-start | bytes 262144 | tf_op jit(solution)/shard_map/all_to_all | solution.py:507
  10.0 0.0 collective-permute-done.refs_0_
  10.1 1.6 %collective-permute-start.2 = (bf16[104,256]{1,0:T(8,128)(2,1)S(1)}, bf16[104,256]{1,0:T(8,128)(2,1)S(1)}, u32[]{:S(2)}, u32[]{:S(2)}) collective-permute-start(bf16[104,256]{1,0:T(8,128)(2,1)S(1)} %get-tuple-element.34), channel_id=1, source_target_pairs={{8,16},{16,8},{24,0},{0,24},{9,17},{17,9},{25,1},{1,25},{10,18},{1... | collective-permute-start | bytes 159752 | tf_op jit(solution)/shard_map/ppermute | solution.py:451
  11.6 0.4 %collective-permute-start.1 = (bf16[104,256]{1,0:T(8,128)(2,1)S(1)}, bf16[104,256]{1,0:T(8,128)(2,1)S(1)}, u32[]{:S(2)}, u32[]{:S(2)}) collective-permute-start(bf16[104,256]{1,0:T(8,128)(2,1)S(1)} %get-tuple-element.30.after), channel_id=1, source_target_pairs={{0,8},{8,0},{16,24},{24,16},{1,9},{9,1},{17,25},{25,17},{2,10},{10... | collective-permute-start | bytes 159752 | tf_op jit(solution)/shard_map/ppermute | solution.py:451
  12.0 1.9 %shard_map.138 = (bf16[256,256]{1,0:T(8,128)(2,1)}, bf16[256,256]{1,0:T(8,128)(2,1)S(1)}, bf16[256,256]{1,0:T(8,128)(2,1)S(1)}, bf16[256,256]{1,0:T(8,128)(2,1)S...) custom-call(bf16[576,256]{1,0:T(8,128)(2,1)S(1)} %get-tuple-element., ...), custom_call_target="tpu_custom_call" | custom-call | tf_op jit(solution)/shard_map/pallas_call | solution.py:57
  13.9 0.3 collective-permute-done.2.from_b
  14.2 0.0 collective-permute-done.1.from_a
  14.2 0.1 shard_map.139
  14.3 2.1 %collective-permute-start.3 = (bf16[136,256]{1,0:T(8,128)(2,1)S(1)}, bf16[136,256]{1,0:T(8,128)(2,1)S(1)}, u32[]{:S(2)}, u32[]{:S(2)}) collective-permute-start(bf16[136,256]{1,0:T(8,128)(2,1)S(1)} %get-tuple-element.36), channel_id=1, source_target_pairs={{0,1},{1,0},{2,3},{3,2},{4,5},{5,4},{6,7},{7,6},{8,9},{9,8},{10,11... | collective-permute-start | bytes 208904 | tf_op jit(solution)/shard_map/ppermute | solution.py:451
  16.4 2.8 %collective-permute-start.4 = (bf16[136,256]{1,0:T(8,128)(2,1)S(1)}, bf16[136,256]{1,0:T(8,128)(2,1)S(1)}, u32[]{:S(2)}, u32[]{:S(2)}) collective-permute-start(bf16[136,256]{1,0:T(8,128)(2,1)S(1)} %get-tuple-element.37), channel_id=1, source_target_pairs={{1,2},{2,1},{3,0},{0,3},{5,6},{6,5},{7,4},{4,7},{9,10},{10,9},{11,... | collective-permute-start | bytes 208904 | tf_op jit(solution)/shard_map/ppermute | solution.py:451
  19.2 0.0 all-to-all-done
  19.2 4.2 %shard_map.140 = (f32[512,256]{1,0:T(8,128)S(1)}, f32[512,256]{1,0:T(8,128)S(1)}, f32[32,256]{1,0:T(8,128)S(1)}, bf16[512,256]{1,0:T(8,128)(2,1)S(1)}, bf16[256,...) custom-call(f32[2,352,128]{2,1,0:T(8,128)S(1)} %get-tuple-element.35.kept.mid_in, ...), custom_call_target="tpu_custom_call" | custom-call | tf_op jit(solution)/shard_map/pallas_call | solution.py:57
  23.3 0.0 collective-permute-done.3.from_a
  23.4 0.0 collective-permute-done.4.from_b
  23.4 4.2 %shard_map.141 = bf16[512,256]{1,0:T(8,128)(2,1)} custom-call(f32[1,256]{1,0:T(1,128)} %bitcast.10, bf16[512,256]{1,0:T(8,128)(2,1)S(1)} %get-tuple-element.31.queries, f32[2,352,128]{2,1,0:T(8,128)S(1)} %get-tuple-element.35.kept.mid_in, bf16[136,256]{1,0:T(8,128)(2,1)S(1)} %collective-permute-done.3.from_a, ...), custom_call_target="tpu_custom_call" | custom-call | tf_op jit(solution)/shard_map/pallas_call | solution.py:57
  (1 shorter events, 0.0 us)
Async XLA Ops:
  2.1 7.9 %collective-permute-start = (bf16[160,256]{1,0:T(8,128)(2,1)S(1)}, bf16[160,256]{1,0:T(8,128)(2,1)S(1)}, u32[]{:S(2)}, u32[]{:S(2)}) collective-permute-start(bf16[160,256]{1,0:T(8,128)(2,1)S(1)} %get-tuple-element.29), channel_id=1, source_target_pairs={{0,4},{4,0},{1,5},{5,1},{2,6},{6,2},{3,7},{7,3},{8,12},{12,8},{9,1... | collective-permute-start | bytes 245768 | tf_op jit(solution)/shard_map/ppermute | solution.py:451
  5.1 14.1 %all-to-all-start = ((bf16[32,8,256]{2,1,0:T(8,128)(2,1)}), bf16[32,8,256]{2,1,0:T(8,128)(2,1)S(1)}, u32[]{:S(2)}, u32[]{:S(2)}) async-start(bf16[32,8,256]{2,1,0:T(8,128)(2,1)} %bitcast.3), calls=%async_computation | async-start | bytes 262144 | tf_op jit(solution)/shard_map/all_to_all | solution.py:507
  10.1 4.1 %collective-permute-start.2 = (bf16[104,256]{1,0:T(8,128)(2,1)S(1)}, bf16[104,256]{1,0:T(8,128)(2,1)S(1)}, u32[]{:S(2)}, u32[]{:S(2)}) collective-permute-start(bf16[104,256]{1,0:T(8,128)(2,1)S(1)} %get-tuple-element.34), channel_id=1, source_target_pairs={{8,16},{16,8},{24,0},{0,24},{9,17},{17,9},{25,1},{1,25},{10,18},{1... | collective-permute-start | bytes 159752 | tf_op jit(solution)/shard_map/ppermute | solution.py:451
  11.6 2.6 %collective-permute-start.1 = (bf16[104,256]{1,0:T(8,128)(2,1)S(1)}, bf16[104,256]{1,0:T(8,128)(2,1)S(1)}, u32[]{:S(2)}, u32[]{:S(2)}) collective-permute-start(bf16[104,256]{1,0:T(8,128)(2,1)S(1)} %get-tuple-element.30.after), channel_id=1, source_target_pairs={{0,8},{8,0},{16,24},{24,16},{1,9},{9,1},{17,25},{25,17},{2,10},{10... | collective-permute-start | bytes 159752 | tf_op jit(solution)/shard_map/ppermute | solution.py:451
  14.3 9.0 %collective-permute-start.3 = (bf16[136,256]{1,0:T(8,128)(2,1)S(1)}, bf16[136,256]{1,0:T(8,128)(2,1)S(1)}, u32[]{:S(2)}, u32[]{:S(2)}) collective-permute-start(bf16[136,256]{1,0:T(8,128)(2,1)S(1)} %get-tuple-element.36), channel_id=1, source_target_pairs={{0,1},{1,0},{2,3},{3,2},{4,5},{5,4},{6,7},{7,6},{8,9},{9,8},{10,11... | collective-permute-start | bytes 208904 | tf_op jit(solution)/shard_map/ppermute | solution.py:451
  16.4 6.9 %collective-permute-start.4 = (bf16[136,256]{1,0:T(8,128)(2,1)S(1)}, bf16[136,256]{1,0:T(8,128)(2,1)S(1)}, u32[]{:S(2)}, u32[]{:S(2)}) collective-permute-start(bf16[136,256]{1,0:T(8,128)(2,1)S(1)} %get-tuple-element.37), channel_id=1, source_target_pairs={{1,2},{2,1},{3,0},{0,3},{5,6},{6,5},{7,4},{4,7},{9,10},{10,9},{11,... | collective-permute-start | bytes 208904 | tf_op jit(solution)/shard_map/ppermute | solution.py:451
